TPU v7x, 512 devices: a whole 4x8x8 slice. The times are simulated.
512 devices in a mesh: dp: 32 (over z, x), expert: 16 (over y, core).
Axes of the slice: x: 4, y: 8, z: 8, core: 2. Of those that a mesh axis runs over, the one named last changes fastest.
Arguments:
- incoming_vectors: bfloat16 [65536, 1024], P(('dp', 'expert')), may hold values from -6 to 6
- widening_matrix_entries: bfloat16 [704, 32, 1024], P('dp', 'expert'), may hold values from -0.1875 to 0.1875
- switch_input_sums: bfloat16 [704, 327680], P(None, ('dp', 'expert')), may hold values from -8 to 8
- inner_adjoint_signal: bfloat16 [704, 327680], P(None, ('dp', 'expert')), may hold values from -16 to 16
- chosen_specialists: int32 [65536, 6], P(('dp', 'expert')), may hold values from 0 to 31, as said below
- assignment_seat_position: int32 [65536, 6], P(('dp', 'expert')), may hold values from 0 to 127, as said below
- admission_quota: int32 [32], replicated, may hold values from 1 to 20, as said below
Outputs:
- token_grad: bfloat16 [65536, 1024], P(('dp', 'expert'))
- muon_update: float32 [704, 32, 1024], P('dp', 'expert')
Inputs may be any that keep to these rules, and one draw needn't show every extreme that they name: `chosen_specialists`: each token names 6 different experts; one expert, which one varies, is named by every token. `assignment_seat_position`: within each aligned block of 128 incoming_vectors (the tokens of one device), the routes to one expert carry the positions 0, 1, ... up to their number minus one, each once. `admission_quota`: the expert named by every token has capacity 20.
All inputs are finite; a program needn't handle non-finite values.
Results may differ from a plain program's by a relative error of at most 0.035.
Values may be sent and summed in bfloat16 or wider, within the bound.
A program may use at most 64 MiB of HBM per device.

v0:
```python
import math

import jax
import jax.numpy as jnp
from jax import lax
from jax.sharding import PartitionSpec as P

ITERS = 2


quint_a = 3.4445
quint_b = -4.775
quint_c = 2.0315
epsilon = 1e-06


def swapped(block, axis, bit):
    count = lax.axis_size(axis)
    route = []
    for low in range(count):
        high = low | 1 << bit
        if high != low and high < count:
            route += [(low, high), (high, low)]
    return lax.ppermute(block, axis, route)


def body(
    incoming_vectors,
    widening_matrix_entries,
    switch_input_sums,
    inner_adjoint_signal,
    chosen_specialists,
    assignment_seat_position,
    admission_quota,
):
    expert_count = lax.axis_size("expert")
    dp_count = lax.axis_size("dp")
    specialist_ordinals = admission_quota.shape[0]
    per_device = specialist_ordinals // expert_count
    slot_cap = switch_input_sums.shape[1] // (expert_count * per_device)
    tok_count = incoming_vectors.shape[0]
    width = incoming_vectors.shape[1]
    hidden = switch_input_sums.shape[0]
    row_share = hidden // dp_count
    slot_total = specialist_ordinals * slot_cap
    specialist_agreement = chosen_specialists[..., None] == jnp.arange(
        specialist_ordinals, dtype=jnp.int32
    )
    quota_ceilings = jnp.sum(jnp.where(specialist_agreement, admission_quota, 0), axis=-1)
    surviving_flags = assignment_seat_position < quota_ceilings
    targets = jnp.where(
        surviving_flags, chosen_specialists * slot_cap + assignment_seat_position, slot_total
    ).reshape(-1)
    owners = jnp.broadcast_to(
        jnp.arange(tok_count, dtype=jnp.int32)[:, None], chosen_specialists.shape
    ).reshape(-1)
    slot_token = jnp.zeros((slot_total + 1,), jnp.int32).at[targets].set(owners)
    filled = (
        jnp.zeros((slot_total + 1,), jnp.bfloat16)
        .at[targets]
        .set(jnp.ones((targets.shape[0],), jnp.bfloat16))
    )
    outgoing = incoming_vectors[slot_token[:slot_total]] * filled[:slot_total, None]
    arrived = lax.all_to_all(outgoing, "expert", split_axis=0, concat_axis=0, tiled=True)
    arrived = arrived.reshape(expert_count, per_device, slot_cap, width)
    up_grad = (
        inner_adjoint_signal.astype(jnp.float32)
        * jax.nn.silu(switch_input_sums.astype(jnp.float32))
    ).astype(jnp.bfloat16)
    grad_grid = up_grad.reshape(hidden, expert_count, per_device, slot_cap)
    section = grad_grid
    slot_grad = jnp.einsum(
        "fjlp,fld->jlpd",
        section,
        lax.all_gather(widening_matrix_entries, "dp", axis=0, tiled=True),
        preferred_element_type=jnp.float32,
    )
    returned = lax.all_to_all(
        slot_grad.astype(jnp.bfloat16).reshape(slot_total, width),
        "expert",
        split_axis=0,
        concat_axis=0,
        tiled=True,
    )
    lookup = jnp.where(surviving_flags, chosen_specialists * slot_cap + assignment_seat_position, 0)
    picked = returned[lookup]
    token_grad = jnp.sum(
        jnp.where(surviving_flags[..., None], picked.astype(jnp.float32), 0.0), axis=1
    ).astype(jnp.bfloat16)
    section = grad_grid
    grad_part = lax.psum_scatter(
        jnp.einsum("fjlp,jlpd->fld", section, arrived, preferred_element_type=jnp.float32).astype(
            jnp.bfloat16
        ),
        "dp",
        scatter_dimension=0,
        tiled=True,
    )
    grad_full = lax.all_gather(grad_part, "dp", axis=0, tiled=True)
    wide = grad_full.astype(jnp.float32)
    norms = jnp.sqrt(jnp.sum(wide * wide, axis=(0, 2), keepdims=True))
    start_iter = (wide / (norms + epsilon)).astype(jnp.bfloat16)
    dp_index = lax.axis_index("dp")
    my_start = dp_index * row_share
    my_matrix = dp_index % 2
    iterate = lax.dynamic_index_in_dim(start_iter, my_matrix, 1, keepdims=False)
    for iteration in range(ITERS):
        gram = lax.dot_general(
            iterate, iterate, (((1,), (1,)), ((), ())), preferred_element_type=jnp.float32
        ).astype(jnp.bfloat16)
        square = jnp.dot(gram, gram, preferred_element_type=jnp.float32)
        poly = (quint_b * gram.astype(jnp.float32) + quint_c * square).astype(jnp.bfloat16)
        iterate = (
            quint_a * iterate.astype(jnp.float32)
            + jnp.dot(poly, iterate, preferred_element_type=jnp.float32)
        ).astype(jnp.bfloat16)
    own_rows = lax.dynamic_slice_in_dim(iterate, my_start, row_share, 0)
    partner = jnp.bitwise_xor(dp_index, 1)
    partner_rows = lax.dynamic_slice_in_dim(iterate, partner * row_share, row_share, 0)
    other_rows = swapped(partner_rows, "dp", 0)
    first_rows = jnp.where(my_matrix == 0, own_rows, other_rows)
    second_rows = jnp.where(my_matrix == 0, other_rows, own_rows)
    final_rows = jnp.stack([first_rows, second_rows], axis=1)
    scale = 0.2 * math.sqrt(max(hidden, width))
    return (token_grad, scale * final_rows.astype(jnp.float32))


def solution(mesh):
    return jax.shard_map(
        body,
        mesh=mesh,
        in_specs=(
            P(("dp", "expert"), None),
            P("dp", "expert", None),
            P(None, ("dp", "expert")),
            P(None, ("dp", "expert")),
            P(("dp", "expert"), None),
            P(("dp", "expert"), None),
            P(),
        ),
        out_specs=(P(("dp", "expert"), None), P("dp", "expert", None)),
        check_vma=False,
    )
```

profile of v0, /device:TPU:6, one launch (start us, length us, event | category | flops | bytes accessed | tf_op | source)
XLA Modules:
  0.0 449.9 jit_solution(7178262200969586018)
XLA Ops:
  7.2 0.8 select_reduce_fusion.1
  8.0 0.7 broadcast_select_fusion
  8.7 0.1 copy.75
  8.8 0.1 reshape.67
  9.0 0.1 reshape.90
  9.2 3.4 scatter_custom_fusion
  12.6 8.6 %scatter_custom_fusion.1 = bf16[641]{0:T(1024)(128)(2,1)S(1)} fusion(s32[768]{0:T(1024)S(1)} %fusion.19, bf16[768]{0:T(1024)(128)(2,1)S(1)} %broadcast.54, bf16[]{:T(256)} %constant.31.clone.1), kind=kCustom, calls=%fused_computation.48 | custom fusion | bytes 1284 | tf_op jit(solution)/shard_map/scatter | solution.py:61
  21.2 0.1 mul.58
  21.3 2.8 gather_fusion.1
  24.2 1.2 broadcast_multiply_fusion
  25.4 7.3 %all-to-all-start.1 = ((bf16[16,40,1024]{2,1,0:T(8,128)(2,1)}), bf16[16,40,1024]{2,1,0:T(8,128)(2,1)S(1)}, u32[]{:S(2)}, u32[]{:S(2)}) async-start(bf16[16,40,1024]{2,1,0:T(8,128)(2,1)} %broadcast_multiply_fusion), calls=%async_computation.1 | async-start | bytes 2621440 | tf_op jit(solution)/shard_map/all_to_all | solution.py:64
  32.7 0.2 all-reduce.3.cloned.1.call-start
  33.0 1.7 fusion.8
  34.7 1.0 copy.69
  35.7 1.2 reshape.66
  36.9 28.0 %all-to-all-done.1 = bf16[16,40,1024]{2,1,0:T(8,128)(2,1)S(1)} async-done(((bf16[16,40,1024]{2,1,0:T(8,128)(2,1)}), bf16[16,40,1024]{2,1,0:T(8,128)(2,1)S(1)}, u32[]{:S(2)}, u32[]{:S(2)}) %all-to-all-start.1) | async-done | bytes 1310752 | tf_op jit(solution)/shard_map/all_to_all | solution.py:64
  64.9 0.7 copy.76
  65.7 1.8 fusion
  67.4 4.6 %copy.78 = bf16[704,2,1024]{2,1,0:T(2,128)(2,1)} copy(bf16[704,2,1024]{2,0,1:T(8,128)(2,1)S(1)} %fusion) | data formatting | bytes 5767168 | tf_op jit(solution)/shard_map/convert_element_type | solution.py:92
  72.0 0.0 all-gather.3.cloned.1.call-start
  72.0 0.7 all-gather.3.cloned.1.call-update
  72.8 0.0 all-gather.5.cloned.1.call-start
  72.8 1.3 dynamic-slice
  74.7 167.3 %all-reduce.3.cloned.1.call-done = bf16[704,2,1024]{2,1,0:T(2,128)(2,1)} async-done(((bf16[704,2,1024]{2,1,0:T(2,128)(2,1)}), bf16[704,2,1024]{2,1,0:T(2,128)(2,1)}) %all-reduce.3.cloned.1.call-update) | async-done | bytes 2883600
  242.0 1.6 constant_dynamic-slice_fusion.1
  243.6 84.1 %all-gather.3.cloned.1.call-done = bf16[704,2,1024]{2,1,0:T(2,128)(2,1)} async-done(((bf16[22,2,1024]{2,1,0:T(2,128)(2,1)}), bf16[704,2,1024]{2,1,0:T(2,128)(2,1)}) %all-gather.3.cloned.1.call-update) | async-done | bytes 2883600 | tf_op jit(solution)/shard_map/all_gather | solution.py:75
  327.8 3.4 fusion.12
  331.2 0.7 copy.72
  331.9 1.8 copy.73
  333.7 7.0 %all-to-all-start = ((bf16[16,40,1024]{2,1,0:T(8,128)(2,1)}), bf16[16,40,1024]{2,1,0:T(8,128)(2,1)S(1)}, u32[]{:S(2)}, u32[]{:S(2)}) async-start(bf16[16,40,1024]{2,1,0:T(8,128)(2,1)} %copy.73), calls=%async_computation | async-start | bytes 2621440 | tf_op jit(solution)/shard_map/all_to_all | solution.py:78
  340.7 0.1 copy.68
  340.9 0.1 copy.74
  341.0 0.1 reshape.72
  341.2 31.7 %all-to-all-done = bf16[16,40,1024]{2,1,0:T(8,128)(2,1)S(1)} async-done(((bf16[16,40,1024]{2,1,0:T(8,128)(2,1)}), bf16[16,40,1024]{2,1,0:T(8,128)(2,1)S(1)}, u32[]{:S(2)}, u32[]{:S(2)}) %all-to-all-start) | async-done | bytes 1310752 | tf_op jit(solution)/shard_map/all_to_all | solution.py:78
  372.9 2.8 gather_fusion
  375.7 2.2 reshape.105
  377.9 36.1 %all-gather.5.cloned.1.call-done = bf16[704,2,1024]{2,1,0:T(2,128)(2,1)} async-done(((bf16[22,2,1024]{2,1,0:T(2,128)(2,1)}), bf16[704,2,1024]{2,1,0:T(2,128)(2,1)}) %all-gather.5.cloned.1.call-update) | async-done | bytes 2883600 | tf_op jit(solution)/shard_map/all_gather | solution.py:99
  414.1 3.0 multiply_reduce_fusion
  417.0 0.6 dynamic-slice.2
  417.6 1.0 copy_convert_fusion
  418.7 2.5 copy-done.2
  421.2 2.0 convolution_convert_fusion.1
  423.1 5.6 %add_convert_fusion.1 = bf16[704,1024]{1,0:T(8,128)(2,1)S(1)} fusion(bf16[704,704]{1,0:T(8,128)(2,1)S(1)} %convolution_convert_fusion.1, f32[1]{0:T(128)} %dynamic-slice.2, f32[704,2,1024]{2,0,1:T(8,128)} %copy-done.2, s32[]{:T(128)S(6)} %select_n.70), kind=kOutput, calls=%fused_computation.14 | convolution fusion | flops 1721094144 | bytes 10455040 | tf_op jit(solution)/shard_map/dot_general | solution.py:115
  428.7 2.3 convolution_convert_fusion
  431.0 4.2 add_convert_fusion
  435.3 2.8 collective-permute-start
  438.1 4.4 select_reduce_fusion
  442.5 0.8 copy.80
  (27 shorter events, 0.2 us)
Async XLA Ops:
  7.2 14.1 %copy-start = (bf16[128,1024]{1,0:T(8,128)(2,1)S(1)}, bf16[128,1024]{1,0:T(8,128)(2,1)}, u32[]{:S(2)}) copy-start(bf16[128,1024]{1,0:T(8,128)(2,1)} %param.7) | copy-start | bytes 786436
  25.4 7.6 %copy-start.4 = (bf16[704,640]{1,0:T(8,128)(2,1)S(1)}, bf16[704,640]{1,0:T(8,128)(2,1)}, u32[]{:S(2)}) copy-start(bf16[704,640]{1,0:T(8,128)(2,1)} %param.9) | copy-start | bytes 2703364
  25.4 39.5 %all-to-all-start.1 = ((bf16[16,40,1024]{2,1,0:T(8,128)(2,1)}), bf16[16,40,1024]{2,1,0:T(8,128)(2,1)S(1)}, u32[]{:S(2)}, u32[]{:S(2)}) async-start(bf16[16,40,1024]{2,1,0:T(8,128)(2,1)} %broadcast_multiply_fusion), calls=%async_computation.1 | async-start | bytes 2621440 | tf_op jit(solution)/shard_map/all_to_all | solution.py:64
  32.7 209.3 %all-reduce.3.cloned.1.call-start = ((), (), s32[]{:S(2)}) async-start(), calls=%async_computation.4 | async-start | bytes 5767168
  36.9 28.8 %copy-start.3 = (bf16[704,16,2,20]{0,3,2,1:T(8,128)(2,1)S(1)}, bf16[704,16,2,20]{0,3,2,1:T(8,128)(2,1)}, u32[]{:S(2)}) copy-start(bf16[704,16,2,20]{0,3,2,1:T(8,128)(2,1)} %reshape.66) | copy-start | bytes 2703364
  72.0 255.8 %all-gather.3.cloned.1.call-start = ((), (), s32[]{:S(2)}) async-start(), calls=%async_computation.2 | async-start | bytes 2973696 | tf_op jit(solution)/shard_map/all_gather | solution.py:75
  72.8 341.3 %all-gather.5.cloned.1.call-start = ((), (), s32[]{:S(2)}) async-start(), calls=%async_computation.3 | async-start | bytes 2973696 | tf_op jit(solution)/shard_map/all_gather | solution.py:99
  333.7 7.2 %copy-start.5 = (s32[128,6]{0,1:T(8,128)S(1)}, s32[128,6]{0,1:T(8,128)}, u32[]{:S(2)}) copy-start(s32[128,6]{0,1:T(8,128)} %param.11) | copy-start | bytes 9220
  333.7 7.2 %copy-start.6 = (s32[128,6]{0,1:T(8,128)S(1)}, s32[128,6]{0,1:T(8,128)}, u32[]{:S(2)}) copy-start(s32[128,6]{0,1:T(8,128)} %param.12) | copy-start | bytes 9220
  333.7 39.2 %all-to-all-start = ((bf16[16,40,1024]{2,1,0:T(8,128)(2,1)}), bf16[16,40,1024]{2,1,0:T(8,128)(2,1)S(1)}, u32[]{:S(2)}, u32[]{:S(2)}) async-start(bf16[16,40,1024]{2,1,0:T(8,128)(2,1)} %copy.73), calls=%async_computation | async-start | bytes 2621440 | tf_op jit(solution)/shard_map/all_to_all | solution.py:78
  414.1 3.6 copy-start.1
  418.7 2.5 copy-start.2
  435.3 7.1 %collective-permute-start = (bf16[22,1024]{1,0:T(8,128)(2,1)S(1)}, bf16[22,1024]{1,0:T(8,128)(2,1)S(1)}, u32[]{:S(2)}, u32[]{:S(2)}) collective-permute-start(bf16[22,1024]{1,0:T(8,128)(2,1)S(1)} %constant_dynamic-slice_fusion), channel_id=1, source_target_pairs={{0,16},{16,0},{32,48},{48,32},{64,80},{80,64},{96,112},{112,96},{1... | collective-permute-start | bytes 135176 | tf_op jit(solution)/shard_map/ppermute | solution.py:24
Sparse Core Ops, SparseCore 0:
  72.1 169.8 all-reduce.2
  245.7 82.0 all-gather.2
  332.0 82.0 all-gather.4
where the time goes:
time: 451 us; the launch traced here: 450 us
  waiting for transfers between devices  348 us (77%)
  local copies, waits for them, and re-layouts  37.5 us (8%)
  matrix products  19.2 us (4%)
  starting transfers between devices  17.4 us (4%)
  between operations  14.7 us (3%)
  other arithmetic  13 us (3%)
    unnamed x4, waiting for transfers between devices  168 us
    all_gather x1, waiting for transfers between devices, body(): lax.all_gather(widening_matrix_entries, 'dp', axis=0, tiled=True)  84.1 us
    all_gather x1, waiting for transfers between devices, body(): grad_full = lax.all_gather(grad_part, 'dp', axis=0, tiled=True)  36.1 us
    all_to_all x1, waiting for transfers between devices, body(): lax.all_to_all(slot_grad.astype(jnp.bfloat16).reshape(slot_total, width),...  31.7 us
    all_to_all x1, waiting for transfers between devices, body(): lax.all_to_all(outgoing, 'expert', split_axis=0, concat_axis=0, tiled=True)  28 us
    dot_general x2, matrix products, body(): jnp.dot(poly, iterate, preferred_element_type=jnp.float32)  9.81 us
  transfers between devices with their start and end apart: 6, of which 5 were waited for; matrix products, arithmetic and copies ran while one was open for 5% of the time, Pallas kernels for 0%

commit v1 on v0

v1 whole, which is shorter than its diff:
```python
import math

import jax
import jax.numpy as jnp
import numpy as np
from jax import lax
from jax.experimental import pallas as pl
from jax.experimental.pallas import tpu as pltpu
from jax.sharding import PartitionSpec as P

MESH = pl.DeviceIdType.MESH
F32 = jnp.float32
BF16 = jnp.bfloat16

ITERS = 2
QUINT_A = 3.4445
QUINT_B = -4.775
QUINT_C = 2.0315
EPSILON = 1e-06

NX, NY, NZ = 4, 8, 8
NE = 2 * NY
FF, D = 704, 1024
TOK, TOP = 128, 6
CAP = 20
SLOTS = 2 * NE * CAP
ROWS = FF // (NX * NZ)
WBLK = 48
SEAT = 24
EM = 2 * NE * SEAT
HALF = FF // 2
PIECE = TOK // 2

UP, DOWN = 0, 1


def layout_tables():
    table = np.full((8, NX * NZ * WBLK), -1, np.int32)
    for j in range(NE):
        for l in range(2):
            for p in range(CAP):
                s = (j * 2 + l) * CAP + p
                table[0, l * (EM // 2) + j * SEAT + p] = s
                table[1, s] = j * WBLK + l * SEAT + p
    for d in range(NX * NZ):
        for l in range(2):
            for i in range(ROWS):
                table[2, d * WBLK + l * ROWS + i] = d * ROWS + i
                table[3, d * WBLK + l * ROWS + i] = l
    return table


def dot(a, b):
    return jnp.dot(a, b, preferred_element_type=F32)


def dot_nt(a, b):
    return lax.dot_general(a, b, (((1,), (1,)), ((), ())), preferred_element_type=F32)


def kernel(
    tok_ref,
    w_ref,
    gate_ref,
    adj_ref,
    chosen_ref,
    seat_ref,
    quota_ref,
    lay_ref,
    out_tok,
    out_mu,
    tokv,
    wst,
    tbl,
    u_ref,
    uem,
    utj,
    ustt,
    slots,
    part,
    fromopp,
    rsum,
    xrecv,
    zsend,
    zown,
    zrecv,
    sg,
    ret,
    grad,
    x0_ref,
    x1_ref,
    gram,
    poly,
    rows_ref,
    fin,
    t_s,
    t_r,
    y_s,
    y_r,
    c_s,
    c_r,
    z_s,
    z_r,
    wx_s,
    wx_r,
    wf_s,
    wf_r,
    opp_s,
    opp_r,
    rel_s,
    rel_r,
    zp_s,
    zp_r,
    ag_s,
    ag_r,
    rt_s,
    rt_r,
    fn_s,
    fn_r,
):
    dp = lax.axis_index("dp")
    me = lax.axis_index("expert")
    x, z = lax.rem(dp, NX), dp // NX
    y, c = me // 2, lax.rem(me, 2)

    def wrap(v, n):
        return lax.rem(v + 2 * n, n)

    def peer(dx=0, dy=0, dz=0, dc=0):
        core = lax.rem(c + dc, 2)
        return (wrap(z + dz, NZ) * NX + wrap(x + dx, NX), wrap(y + dy, NY) * 2 + core)

    def copy(ref_src, ref_dst, ssem, rsem, device):
        return pltpu.make_async_remote_copy(
            src_ref=ref_src,
            dst_ref=ref_dst,
            send_sem=ssem,
            recv_sem=rsem,
            device_id=device,
            device_id_type=MESH,
        )

    def aligned(v, m):
        return pl.multiple_of(v, m)

    barrier = pltpu.get_barrier_semaphore()
    greeted = [(dp, lax.rem(me + i, NE)) for i in range(1, NE)]
    greeted += [peer(dz=k) for k in range(1, NZ)]
    greeted += [peer(dx=k) for k in range(1, NX)]
    for device in greeted:
        pl.semaphore_signal(barrier, inc=1, device_id=device, device_id_type=MESH)

    chosen = chosen_ref[...]
    quota = jnp.zeros_like(chosen)
    for e in range(2 * NE):
        quota = jnp.where(chosen == e, quota_ref[e], quota)
    code = jnp.where(seat_ref[...] < quota, chosen * 32 + seat_ref[...], -1)
    tbl[me, 0:TOP, :] = code
    tbl[me, TOP:8, :] = jnp.full((8 - TOP, TOK), -1, jnp.int32)

    def tok_rows(yb, cb, p):
        return pl.ds(aligned(yb * (2 * TOK) + cb * TOK + p * PIECE, PIECE), PIECE)

    own_rows = pl.ds(aligned(y * (2 * TOK) + c * TOK, TOK), TOK)
    tokv[own_rows, :] = tok_ref[...]

    def w_rows(zb, xb):
        return pl.ds(aligned((zb * NX + xb) * WBLK, WBLK), WBLK)

    wst[w_rows(z, x), :] = w_ref[...]

    pl.semaphore_wait(barrier, len(greeted))

    sent = []

    def start(cp):
        cp.start()
        sent.append(cp)

    rel = [0, -1, 1, -2, 2, -3, 3, 4]

    def y_copy(direction, hop, p):
        step = 1 if direction == UP else -1
        yb = wrap(y - step * (hop - 1), NY)
        view = tokv.at[tok_rows(yb, c, p), :]
        at = (direction, hop - 1, p)
        return copy(view, view, y_s.at[at], y_r.at[at], peer(dy=step))

    def y_arrival(direction, hop, p):
        step = 1 if direction == UP else -1
        yb = wrap(y - step * hop, NY)
        view = tokv.at[tok_rows(yb, c, p), :]
        at = (direction, hop - 1, p)
        return yb, copy(view, view, y_s.at[at], y_r.at[at], peer(dy=step))

    def to_sibling(n, p):
        yb = wrap(y + rel[n], NY)
        view = tokv.at[tok_rows(yb, c, p), :]
        start(copy(view, view, c_s.at[n, p], c_r.at[n, p], peer(dc=1)))

    def y_recv(direction, hop, p):
        _, cp = y_arrival(direction, hop, p)
        cp.wait_recv()
        if hop < 3 or (hop == 3 and p == direction):
            start(y_copy(direction, hop + 1, p))
        step = 1 if direction == UP else -1
        n = rel.index(-step * hop) if hop < 4 else 7
        to_sibling(n, p)

    left, right = slice(0, D // 2), slice(D // 2, D)

    def z_view(zb, xb, hop, direction):
        if hop < 4:
            return wst.at[w_rows(zb, xb), :]
        return wst.at[w_rows(zb, xb), left if direction == UP else right]

    def z_copy(direction, hop):
        step = 1 if direction == UP else -1
        zb = wrap(z - step * (hop - 1), NZ)
        view = z_view(zb, x, hop, direction)
        at = (direction, hop - 1)
        return copy(view, view, z_s.at[at], z_r.at[at], peer(dz=step))

    def x_sends(n):
        zb = wrap(z + rel[n], NZ)
        view = wst.at[w_rows(zb, x), :]
        for direction, step in ((UP, 1), (DOWN, -1)):
            at = (direction, n)
            start(copy(view, view, wx_s.at[at], wx_r.at[at], peer(dx=step)))

    def z_recv(hop):
        for direction, step in ((UP, 1), (DOWN, -1)):
            zb = wrap(z - step * hop, NZ)
            view = z_view(zb, x, hop, direction)
            at = (direction, hop - 1)
            copy(view, view, z_s.at[at], z_r.at[at], peer(dz=step)).wait_recv()
            if hop < 4:
                start(z_copy(direction, hop + 1))
                x_sends(rel.index(-step * hop))
        if hop == 4:
            x_sends(7)

    def x_recv(n):
        zb = wrap(z + rel[n], NZ)
        for direction, step in ((UP, 1), (DOWN, -1)):
            rows = w_rows(zb, wrap(x - step, NX))
            at = (direction, n)
            view = wst.at[rows, :]
            copy(view, view, wx_s.at[at], wx_r.at[at], peer(dx=step)).wait_recv()
            view = wst.at[rows, left if direction == UP else right]
            start(copy(view, view, wf_s.at[at], wf_r.at[at], peer(dx=step)))

    def xf_wait(n):
        zb = wrap(z + rel[n], NZ)
        rows = w_rows(zb, wrap(x + 2, NX))
        for direction, step in ((UP, 1), (DOWN, -1)):
            at = (direction, n)
            view = wst.at[rows, left if direction == UP else right]
            copy(view, view, wf_s.at[at], wf_r.at[at], peer(dx=step)).wait_recv()

    def up_grad():
        def tile(t, carry):
            rows = pl.ds(aligned(t * 64, 64), 64)
            g = gate_ref[rows, :].astype(F32)
            a = adj_ref[rows, :].astype(F32)
            u_ref[rows, :] = (a * (g / (1.0 + jnp.exp(-g)))).astype(BF16)
            return carry

        lax.fori_loop(0, FF // 64, tile, 0)

    def expert_major():
        pick = jnp.where(
            lax.broadcasted_iota(jnp.int32, (SLOTS, EM), 0) == lay_ref[0:1, 0:EM], 1.0, 0.0
        ).astype(BF16)
        for t in range(2):
            rows = slice(t * HALF, (t + 1) * HALF)
            uem[rows, :] = dot(u_ref[rows, :], pick).astype(BF16)

    def source_major():
        pick = jnp.where(
            lax.broadcasted_iota(jnp.int32, (EM, SLOTS), 0) == lay_ref[1:2, 0:SLOTS], 1.0, 0.0
        ).astype(BF16)
        utj[...] = dot_nt(pick, u_ref[...]).astype(BF16)

    def stacked(t):
        cols = slice(t * 512, (t + 1) * 512)
        pick = jnp.where(
            lax.broadcasted_iota(jnp.int32, (FF, 512), 0) == lay_ref[2:3, cols], 1.0, 0.0
        ).astype(BF16)
        which = lay_ref[3:4, cols]
        local = lax.broadcasted_iota(jnp.int32, (2 * WBLK, 512), 0)
        row_expert = jnp.where(
            local < WBLK, jnp.where(local < SEAT, 0, 1), jnp.where(local < WBLK + SEAT, 0, 1)
        )
        keep = row_expert == which
        full = dot(utj[...], pick)
        for s in range(EM // (2 * WBLK)):
            rows = slice(s * 2 * WBLK, (s + 1) * 2 * WBLK)
            ustt[rows, cols] = jnp.where(keep, full[rows, :], 0.0).astype(BF16)

    def one_hot(yb, cb, l):
        want = lax.broadcasted_iota(jnp.int32, (SEAT, TOK), 0) + (2 * me + l) * 32
        codes = tbl[yb * 2 + cb]
        hit = jnp.zeros((SEAT, TOK), F32)
        for k in range(TOP):
            hit = hit + jnp.where(codes[k : k + 1, :] == want, 1.0, 0.0)
        return hit

    def gather(n):
        yb = wrap(y + rel[n], NY)
        for p in range(2):
            view = tokv.at[tok_rows(yb, 1 - c, p), :]
            copy(view, view, c_s.at[n, p], c_r.at[n, p], peer(dc=1)).wait_recv()
        zero = jnp.zeros((SEAT, TOK), F32)
        blocks = []
        for l in range(2):
            blocks.append(jnp.concatenate([one_hot(yb, 0, l), zero], axis=1))
            blocks.append(jnp.concatenate([zero, one_hot(yb, 1, l)], axis=1))
        pick = jnp.concatenate(blocks, axis=0).astype(BF16)
        tokens = tokv[pl.ds(aligned(yb * 2 * TOK, 2 * TOK), 2 * TOK), :]
        got = dot(pick, tokens).astype(BF16)
        rows = pl.ds(aligned(yb * 2 * SEAT, 2 * SEAT), 2 * SEAT)
        slots[0, rows, :] = got[0 : 2 * SEAT, :]
        slots[1, rows, :] = got[2 * SEAT :, :]

    for i in range(1, NE):
        j = lax.rem(me + i, NE)
        start(copy(tbl.at[me], tbl.at[me], t_s.at[i], t_r.at[i], (dp, j)))
    for p in range(2):
        for direction in (UP, DOWN):
            start(y_copy(direction, 1, p))
    for direction in (UP, DOWN):
        start(z_copy(direction, 1))
    x_sends(0)
    for p in range(2):
        to_sibling(0, p)

    def y_both(hop, p):
        y_recv(UP, hop, p)
        y_recv(DOWN, hop, p)

    up_grad()
    y_both(1, 0)
    z_recv(1)
    x_recv(0)
    expert_major()
    y_both(1, 1)
    x_recv(1)
    source_major()
    y_both(2, 0)
    z_recv(2)
    x_recv(2)
    stacked(0)
    y_both(2, 1)
    x_recv(3)
    for i in range(1, NE):
        j = lax.rem(me + NE - i, NE)
        copy(tbl.at[j], tbl.at[j], t_s.at[i], t_r.at[i], (dp, j)).wait_recv()
    gather(0)
    gather(1)
    y_both(3, 0)
    z_recv(3)
    gather(2)
    stacked(1)
    x_recv(4)
    y_both(3, 1)
    z_recv(4)
    stacked(2)
    gather(3)
    x_recv(5)
    gather(4)
    y_recv(UP, 4, 0)
    y_recv(DOWN, 4, 1)
    gather(5)
    gather(6)
    gather(7)

    r0 = wrap(x - 2 * c, NX)
    is_owner = r0 < 2
    l_other = lax.rem(r0, 2)
    l_relay = 1 - l_other
    is_plus = jnp.logical_or(r0 == 1, r0 == 2)
    b_relay = jnp.where(is_plus, 0, 1)
    h_direct = jnp.where(is_plus, HALF, 0)
    h_sum = HALF - h_direct
    toward = jnp.where(is_plus, -1, 1)
    owner_dev = peer(dx=toward)
    opp_dev = peer(dx=-toward)
    z2 = z // 2
    order = [wrap(z2 + k, 4) for k in (2, 1, 3, 0)]

    def cols2(i):
        return pl.ds(aligned(order[i] * 256, 256), 256)

    def halfrows(h):
        return pl.ds(aligned(h, HALF), HALF)

    def direct_copy(i):
        return copy(
            part.at[l_relay, halfrows(h_direct), cols2(i)],
            xrecv.at[b_relay, halfrows(h_direct), cols2(i)],
            rel_s.at[0, i],
            rel_r.at[b_relay, 0, i],
            owner_dev,
        )

    def summed_copy(i):
        return copy(
            rsum.at[:, cols2(i)],
            xrecv.at[b_relay, halfrows(h_sum), cols2(i)],
            rel_s.at[1, i],
            rel_r.at[b_relay, 1, i],
            owner_dev,
        )

    def opp_copy(i, h):
        return copy(
            part.at[l_other, pl.ds(h * HALF, HALF), cols2(i)],
            fromopp.at[:, cols2(i)],
            opp_s.at[h, i],
            opp_r.at[i],
            peer(dx=-1 if h == 0 else 1),
        )

    def partials(i):
        for l in range(2):
            right_side = slots[l, :, cols2(i)]
            for t in range(2):
                rows = slice(t * HALF, (t + 1) * HALF)
                part[l, rows, cols2(i)] = dot(
                    uem[rows, l * (EM // 2) : (l + 1) * (EM // 2)], right_side
                ).astype(BF16)
        start(direct_copy(i))

        @pl.when(jnp.logical_not(is_owner))
        def _():
            opp_copy(i, 0).start()
            opp_copy(i, 1).start()

    def relay(i):
        opp = fromopp.at[:, cols2(i)]
        copy(opp, opp, opp_s.at[0, i], opp_r.at[i], opp_dev).wait_recv()
        rsum[:, cols2(i)] = (
            part[l_relay, halfrows(h_sum), cols2(i)].astype(F32) + fromopp[:, cols2(i)].astype(F32)
        ).astype(BF16)
        start(summed_copy(i))

    def z_part(i, k):
        zeta = order[i] * 2 + k
        view = zsend.at[:, pl.ds(aligned(zeta * 128, 128), 128)]
        return copy(view, zrecv.at[z], zp_s.at[i, k], zp_r.at[z], (zeta * NX + x, me))

    def finish(i):
        @pl.when(is_owner)
        def _():
            for b in range(2):
                for kind in range(2):
                    h = (1 - b) * HALF if kind == 0 else b * HALF
                    view = xrecv.at[b, pl.ds(h, HALF), cols2(i)]
                    copy(
                        view, view, rel_s.at[0, i], rel_r.at[b, kind, i], peer(dx=1 if b == 0 else -1)
                    ).wait_recv()
            total = (
                part[l_other, :, cols2(i)].astype(F32)
                + xrecv[0, :, cols2(i)].astype(F32)
                + xrecv[1, :, cols2(i)].astype(F32)
            )
            zsend[:, cols2(i)] = total.astype(BF16)
            if i < 3:
                z_part(i, 0).start()
                z_part(i, 1).start()
            else:

                @pl.when(lax.rem(z, 2) == 0)
                def _():
                    z_part(i, 1).start()
                    zown[...] = total[:, 0:128]

                @pl.when(lax.rem(z, 2) == 1)
                def _():
                    z_part(i, 0).start()
                    zown[...] = total[:, 128:256]

    def slot_grads(n):
        cols = slice(n * 256, (n + 1) * 256)
        sg[:, cols] = dot(ustt[...], wst[:, cols]).astype(BF16)

    def block_rows(j):
        return pl.ds(aligned(j * WBLK, WBLK), WBLK)

    partials(0)
    partials(1)
    x_recv(6)
    x_recv(7)
    relay(0)
    partials(2)
    relay(1)
    partials(3)
    for n in range(8):
        xf_wait(n)
    slot_grads(0)
    finish(0)
    slot_grads(1)
    relay(2)
    slot_grads(2)
    finish(1)
    slot_grads(3)
    for i in range(1, NE):
        j = lax.rem(me + i, NE)
        start(
            copy(
                sg.at[block_rows(j), :],
                ret.at[block_rows(me), :],
                rt_s.at[i],
                rt_r.at[i],
                (dp, j),
            )
        )
    ret[block_rows(me), :] = sg[block_rows(me), :]
    relay(3)
    finish(2)
    finish(3)

    zcols = pl.ds(aligned(z * 128, 128), 128)

    def ag_view(zb, p):
        return grad.at[pl.ds(p * HALF, HALF), pl.ds(aligned(zb * 128, 128), 128)]

    def ag_copy(direction, hop, p):
        step = 1 if direction == UP else -1
        view = ag_view(wrap(z - step * (hop - 1), NZ), p)
        at = (direction, hop - 1, p)
        return copy(view, view, ag_s.at[at], ag_r.at[at], peer(dz=step))

    def ag_recv(direction, hop, p):
        step = 1 if direction == UP else -1
        view = ag_view(wrap(z - step * hop, NZ), p)
        at = (direction, hop - 1, p)
        copy(view, view, ag_s.at[at], ag_r.at[at], peer(dz=step)).wait_recv()
        if hop < 3 or (hop == 3 and p == direction):
            ag_copy(direction, hop + 1, p).start()

    def rows_copy(k):
        xd = wrap(x + k, NX)
        return copy(
            rows_ref.at[pl.ds(aligned(xd * 32, 32), 32), :],
            fin.at[l_other],
            fn_s.at[k],
            fn_r.at[l_other],
            peer(dx=k),
        )

    @pl.when(is_owner)
    def _():
        total = zown[...]
        for k in range(1, NZ):
            src = wrap(z + k, NZ)
            view = zrecv.at[src]
            copy(view, view, zp_s.at[0, 0], zp_r.at[src], peer(dz=k)).wait_recv()
            total = total + zrecv[src].astype(F32)
        grad[:, zcols] = total.astype(BF16)
        for p in range(2):
            for direction in (UP, DOWN):
                ag_copy(direction, 1, p).start()
        for hop in range(1, 4):
            for p in range(2):
                for direction in (UP, DOWN):
                    ag_recv(direction, hop, p)
        ag_recv(UP, 4, 0)
        ag_recv(DOWN, 4, 1)

        wide = grad[...].astype(F32)
        squares = jnp.sum(jnp.sum(wide * wide, axis=0, keepdims=True), axis=1, keepdims=True)
        inverse = 1.0 / (jnp.sqrt(squares) + EPSILON)
        x0_ref[...] = (wide * inverse).astype(BF16)

        halves = [slice(0, HALF), slice(HALF, FF)]

        def grams(it):
            for rows in halves:
                gram[rows, :] = dot_nt(it[rows, :], it[...]).astype(BF16)

        grams(x0_ref)
        for rows in halves:
            square = dot(gram[rows, :], gram[...])
            poly[rows, :] = (QUINT_B * gram[rows, :].astype(F32) + QUINT_C * square).astype(BF16)
        for rows in halves:
            x1_ref[rows, :] = (
                QUINT_A * x0_ref[rows, :].astype(F32) + dot(poly[rows, :], x0_ref[...])
            ).astype(BF16)
        grams(x1_ref)
        picks = []
        for xd in range(NX):
            r = lax.broadcasted_iota(jnp.int32, (32, FF), 0)
            f = lax.broadcasted_iota(jnp.int32, (32, FF), 1)
            hit = jnp.logical_and(r < ROWS, f == r + (z * NX + xd) * ROWS)
            picks.append(jnp.where(hit, 1.0, 0.0))
        pick = jnp.concatenate(picks, axis=0).astype(BF16)
        gram_rows = dot(pick, gram[...]).astype(BF16)
        it_rows = dot(pick, x1_ref[...])
        poly_rows = (QUINT_B * gram_rows.astype(F32) + QUINT_C * dot(gram_rows, gram[...])).astype(
            BF16
        )
        rows_ref[...] = (QUINT_A * it_rows + dot(poly_rows, x1_ref[...])).astype(BF16)
        for k in range(1, NX):
            rows_copy(k).start()
        fin[l_other] = rows_ref[pl.ds(aligned(x * 32, 32), 32), :]

    for i in range(1, NE):
        j = lax.rem(me + NE - i, NE)
        view = ret.at[block_rows(j), :]
        copy(view, view, rt_s.at[i], rt_r.at[i], (dp, j)).wait_recv()
    hits = []
    for e in range(2 * NE):
        want = lax.broadcasted_iota(jnp.int32, (SEAT, TOK), 0) + e * 32
        hit = jnp.zeros((SEAT, TOK), F32)
        for k in range(TOP):
            hit = hit + jnp.where(code[k : k + 1, :] == want, 1.0, 0.0)
        hits.append(hit)
    pick = jnp.concatenate(hits, axis=0).T.astype(BF16)
    out_tok[...] = dot(pick, ret[...]).astype(BF16)

    scale = 0.2 * math.sqrt(max(FF, D))
    for l in range(2):
        owner_x = 2 * c + l

        @pl.when(x != owner_x)
        def _():
            view = fin.at[l]
            copy(view, view, fn_s.at[1], fn_r.at[l], peer(dx=1)).wait_recv()

        out_mu[:, l, :] = scale * fin[l, 0:ROWS, :].astype(F32)

    for cp in sent:
        cp.wait_send()

    @pl.when(jnp.logical_not(is_owner))
    def _():
        for i in range(4):
            opp_copy(i, 0).wait_send()
            opp_copy(i, 1).wait_send()

    @pl.when(is_owner)
    def _():
        for i in range(3):
            z_part(i, 0).wait_send()
            z_part(i, 1).wait_send()

        @pl.when(lax.rem(z, 2) == 0)
        def _():
            z_part(3, 1).wait_send()

        @pl.when(lax.rem(z, 2) == 1)
        def _():
            z_part(3, 0).wait_send()

        for hop in range(1, 5):
            for p in range(2):
                for direction in (UP, DOWN):
                    if hop < 4 or p == direction:
                        ag_copy(direction, hop, p).wait_send()
        for k in range(1, NX):
            rows_copy(k).wait_send()


def body(tokens, weights, gate, adjoint, chosen, seat, quota):
    stacked_w = jnp.concatenate(
        [weights[:, 0, :], weights[:, 1, :], jnp.zeros((WBLK - 2 * ROWS, D), BF16)], axis=0
    )
    vmem = pl.BlockSpec(memory_space=pltpu.VMEM)
    sem = pltpu.SemaphoreType.DMA
    scratch = [
        pltpu.VMEM((NE * TOK, D), BF16),
        pltpu.VMEM((NX * NZ * WBLK, D), BF16),
        pltpu.VMEM((NE, 8, TOK), jnp.int32),
        pltpu.VMEM((FF, SLOTS), BF16),
        pltpu.VMEM((FF, EM), BF16),
        pltpu.VMEM((EM, FF), BF16),
        pltpu.VMEM((EM, NX * NZ * WBLK), BF16),
        pltpu.VMEM((2, EM // 2, D), BF16),
        pltpu.VMEM((2, FF, D), BF16),
        pltpu.VMEM((HALF, D), BF16),
        pltpu.VMEM((HALF, D), BF16),
        pltpu.VMEM((2, FF, D), BF16),
        pltpu.VMEM((FF, D), BF16),
        pltpu.VMEM((FF, 128), F32),
        pltpu.VMEM((NZ, FF, 128), BF16),
        pltpu.VMEM((EM, D), BF16),
        pltpu.VMEM((EM, D), BF16),
        pltpu.VMEM((FF, D), BF16),
        pltpu.VMEM((FF, D), BF16),
        pltpu.VMEM((FF, D), BF16),
        pltpu.VMEM((FF, FF), BF16),
        pltpu.VMEM((FF, FF), BF16),
        pltpu.VMEM((128, D), BF16),
        pltpu.VMEM((2, 32, D), BF16),
        sem((NE,)),
        sem((NE,)),
        sem((2, 4, 2)),
        sem((2, 4, 2)),
        sem((8, 2)),
        sem((8, 2)),
        sem((2, 4)),
        sem((2, 4)),
        sem((2, 8)),
        sem((2, 8)),
        sem((2, 8)),
        sem((2, 8)),
        sem((2, 4)),
        sem((4,)),
        sem((2, 4)),
        sem((2, 2, 4)),
        sem((4, 2)),
        sem((NZ,)),
        sem((2, 4, 2)),
        sem((2, 4, 2)),
        sem((NE,)),
        sem((NE,)),
        sem((NX,)),
        sem((2,)),
    ]
    return pl.pallas_call(
        kernel,
        out_shape=(
            jax.ShapeDtypeStruct((TOK, D), BF16),
            jax.ShapeDtypeStruct((ROWS, 2, D), F32),
        ),
        in_specs=[vmem] * 6 + [pl.BlockSpec(memory_space=pltpu.SMEM), vmem],
        out_specs=(vmem, vmem),
        scratch_shapes=scratch,
        compiler_params=pltpu.CompilerParams(
            collective_id=0, has_side_effects=True, vmem_limit_bytes=60 * 2**20
        ),
        cost_estimate=pl.CostEstimate(
            flops=16 * 10**9, bytes_accessed=5 * 10**6, transcendentals=450560
        ),
        name="expert_backward",
    )(tokens, stacked_w, gate, adjoint, chosen.T, seat.T, quota, jnp.asarray(layout_tables()))


def solution(mesh):
    return jax.shard_map(
        body,
        mesh=mesh,
        in_specs=(
            P(("dp", "expert"), None),
            P("dp", "expert", None),
            P(None, ("dp", "expert")),
            P(None, ("dp", "expert")),
            P(("dp", "expert"), None),
            P(("dp", "expert"), None),
            P(),
        ),
        out_specs=(P(("dp", "expert"), None), P("dp", "expert", None)),
        check_vma=False,
    )
```

time: 451 us -> 115 us (0.25)
  waiting for transfers between devices: 348 us -> 0 us
  Pallas kernels: 0 us -> 110 us
  local copies, waits for them, and re-layouts: 37.5 us -> 3.62 us
  matrix products: 19.2 us -> 0 us
  starting transfers between devices: 17.4 us -> 0 us
  between operations: 14.7 us -> 0.66 us
  other arithmetic: 13 us -> 0.72 us
    unnamed x4 -> x0, waiting for transfers between devices: 168 us -> none
    all_gather x2 -> x0, waiting for transfers between devices: 120 us -> none  [the longest x1 84.1 us: body(): lax.all_gather(widening_matrix_entries, 'dp', axis=0, tiled=True)]
    pallas_call x0 -> x1, Pallas kernels: none -> 110 us  [body(): pl.pallas_call(kernel, out_shape=(jax.ShapeDtypeStruct((TOK, D), BF16), j...]
    all_to_all x2 -> x0, waiting for transfers between devices: 59.8 us -> none  [the longest x1 31.7 us: body(): lax.all_to_all(slot_grad.astype(jnp.bfloat16).reshape(slot_total, width),...]
    dot_general x6 -> x0, matrix products: 19.2 us -> none  [the longest x2 9.81 us: body(): jnp.dot(poly, iterate, preferred_element_type=jnp.float32)]
    all_to_all x2 -> x0, starting transfers between devices: 14.3 us -> none  [the longest x1 7.34 us: body(): lax.all_to_all(outgoing, 'expert', split_axis=0, concat_axis=0, tiled=True)]
    scatter x2 -> x0, local copies, waits for them, and re-layouts: 12 us -> none  [the longest x1 8.61 us: body(): filled = jnp.zeros((slot_total + 1,), jnp.bfloat16).at[targets].set(jnp.o...]
    convert_element_type x4 -> x0, local copies, waits for them, and re-layouts: 8.53 us -> none  [the longest x1 4.55 us: body(): jnp.einsum('fjlp,jlpd->fld', section, arrived, preferred_element_type=jnp...]
  transfers between devices with their start and end apart: 6 -> 0, of which waited for: 5 -> 0; matrix products, arithmetic and copies ran while one was open for 5% -> 0% of each run, Pallas kernels for 0% -> 0%
where the time goes in v1:
time: 115 us
  Pallas kernels  110 us (96%)
  local copies, waits for them, and re-layouts  3.62 us (3%)
    pallas_call x1, Pallas kernels, body(): pl.pallas_call(kernel, out_shape=(jax.ShapeDtypeStruct((TOK, D), BF16), j...  110 us
    unnamed x4, local copies, waits for them, and re-layouts  2.38 us

profile of v1, /device:TPU:6, one launch (start us, length us, event | category | flops | bytes accessed | tf_op | source)
XLA Modules:
  0.0 114.9 jit_solution(9392745560743212896)
XLA Ops:
  0.6 0.1 pad.2.clone
  0.7 1.1 fusion
  1.9 0.7 maximum_maximum_fusion.w_ref
  2.6 109.8 %expert_backward.1 = (bf16[128,1024]{1,0:T(8,128)(2,1)}, f32[22,2,1024]{2,1,0:T(2,128)}) custom-call(bf16[128,1024]{1,0:T(8,128)(2,1)} %tok_ref.1, bf16[48,1024]{1,0:T(8,128)(2,1)} %maximum_maximum_fusion.w_ref, bf16[704,640]{1,0:T(8,128)(2,1)} %gate_ref.1, bf16[704,640]{1,0:T(8,128)(2,1)} %adj_ref.1, s32[6,128]{1,0:T(8,128)} %bitcast.6, s32[6,128]{1,0:T(8,128)} %bitcast.7, ...), custom_call_target="tpu_custom_call" | custom-call | flops 16000000000 | bytes 5000000 | tf_op jit(solution)/shard_map/expert_backward/pallas_call | solution.py:722
  112.5 0.0 copy-start
  112.5 1.7 %copy.18 = bf16[128,1024]{1,0:T(8,128)(2,1)} copy(bf16[128,1024]{1,0:T(8,128)(2,1)} %get-tuple-element.8) | data formatting | bytes 524288
  114.2 0.0 copy-done
  114.2 0.7 copy.19
  (2 shorter events, 0.0 us)
Async XLA Ops:
  112.5 1.7 %copy-start = (f32[22,2,1024]{2,1,0:T(2,128)S(1)}, f32[22,2,1024]{2,1,0:T(2,128)}, u32[]{:S(2)}) copy-start(f32[22,2,1024]{2,1,0:T(2,128)} %get-tuple-element.9) | copy-start | bytes 540676

commit v2 on v1

v2 whole, which is shorter than its diff:
```python
import math

import jax
import jax.numpy as jnp
import numpy as np
from jax import lax
from jax.experimental import pallas as pl
from jax.experimental.pallas import tpu as pltpu
from jax.sharding import PartitionSpec as P

MESH = pl.DeviceIdType.MESH
F32 = jnp.float32
BF16 = jnp.bfloat16

ITERS = 2
QUINT_A = 3.4445
QUINT_B = -4.775
QUINT_C = 2.0315
EPSILON = 1e-06

NX, NY, NZ = 4, 8, 8
NE = 2 * NY
FF, D = 704, 1024
TOK, TOP = 128, 6
CAP = 20
SLOTS = 2 * NE * CAP
ROWS = FF // (NX * NZ)
WBLK = 48
GROUP = 4 * CAP
SLOTS_E = NE * CAP
DEPTH = 384
WROWS = 2 * ROWS
ZBLK = NX * WROWS
WALL = NZ * ZBLK
ZPIECES = ((0, 96), (96, ZBLK - 96))
REL = (0, -1, 1, -2, 2, -3, 3, 4)
HALF = FF // 2
PIECE = TOK // 2

UP, DOWN = 0, 1


def layout_tables():
    table = np.full((8, WALL), -1, np.int32)
    table[1, :] = -(1 << 20)
    for n in range(NY):
        for core in range(2):
            for p in range(CAP):
                at = (n * 2 + core) * CAP + p
                table[0, at] = REL[n] % NY
                table[1, at] = core * 2 * CAP + p
    for j in range(NE):
        for l in range(2):
            for p in range(CAP):
                table[2, (j * 2 + l) * CAP + p] = l
    for d in range(NX * NZ):
        for l in range(2):
            for i in range(ROWS):
                table[3, d * WROWS + l * ROWS + i] = d * ROWS + i
                table[4, d * WROWS + l * ROWS + i] = l
    for k in range(NX):
        for i in range(WROWS):
            table[5, k * WBLK + i] = k * WROWS + i
    return table


def dot(a, b):
    return jnp.dot(a, b, preferred_element_type=F32)


def dot_nt(a, b):
    return lax.dot_general(a, b, (((1,), (1,)), ((), ())), preferred_element_type=F32)


def kernel(
    tok_hbm,
    w_hbm,
    gate_hbm,
    adj_hbm,
    chosen_hbm,
    seat_hbm,
    quota_ref,
    lay_hbm,
    out_tok,
    out_mu,
    w_ref,
    gate_ref,
    adj_ref,
    chosen_ref,
    seat_ref,
    lay_ref,
    in_s,
    tokv,
    wx,
    wst,
    tbl,
    u_ref,
    uown,
    utail,
    utails,
    ucat,
    utj,
    ustt,
    sown,
    scat,
    zsend,
    zown,
    zrecv,
    sg,
    ret,
    grad,
    x1_ref,
    gram_sum,
    gram,
    poly,
    rows_ref,
    fin,
    t_s,
    t_r,
    y_s,
    y_r,
    c_s,
    c_r,
    w_s,
    w_r,
    z_s,
    z_r,
    uc_s,
    uc_r,
    sc_s,
    sc_r,
    zp_s,
    zp_r,
    ag_s,
    ag_r,
    rt_s,
    rt_r,
    fn_s,
    fn_r,
    picked,
    for_sibling,
    from_sibling,
    sib_s,
    sib_r,
):
    dp = lax.axis_index("dp")
    me = lax.axis_index("expert")
    x, z = lax.rem(dp, NX), dp // NX
    y, c = me // 2, lax.rem(me, 2)

    def wrap(v, n):
        return lax.rem(v + 2 * n, n)

    def peer(dx=0, dy=0, dz=0, dc=0):
        core = lax.rem(c + dc, 2)
        return (wrap(z + dz, NZ) * NX + wrap(x + dx, NX), wrap(y + dy, NY) * 2 + core)

    def copy(ref_src, ref_dst, ssem, rsem, device):
        return pltpu.make_async_remote_copy(
            src_ref=ref_src,
            dst_ref=ref_dst,
            send_sem=ssem,
            recv_sem=rsem,
            device_id=device,
            device_id_type=MESH,
        )

    def aligned(v, m):
        return pl.multiple_of(v, m)

    barrier = pltpu.get_barrier_semaphore()
    greeted = [(dp, lax.rem(me + i, NE)) for i in range(1, NE)]
    greeted += [peer(dz=k) for k in range(1, NZ)]
    greeted += [peer(dx=k) for k in range(1, NX)]
    for device in greeted:
        pl.semaphore_signal(barrier, inc=1, device_id=device, device_id_type=MESH)

    own_rows = pl.ds(aligned(y * (2 * TOK) + c * TOK, TOK), TOK)
    operands = (
        (tok_hbm, tokv.at[own_rows, :]),
        (w_hbm, w_ref),
        (chosen_hbm, chosen_ref),
        (seat_hbm, seat_ref),
        (lay_hbm, lay_ref),
        (gate_hbm, gate_ref),
        (adj_hbm, adj_ref),
    )
    loads = [pltpu.make_async_copy(a, b, in_s.at[i]) for i, (a, b) in enumerate(operands)]
    for cp in loads:
        cp.start()
    for cp in loads[:4]:
        cp.wait()

    chosen = chosen_ref[...]
    quota = jnp.zeros_like(chosen)
    for e in range(2 * NE):
        quota = jnp.where(chosen == e, quota_ref[e], quota)
    code = jnp.where(seat_ref[...] < quota, chosen * 32 + seat_ref[...], -1)
    tbl[me, 0:TOP, :] = code
    tbl[me, TOP:8, :] = jnp.full((8 - TOP, TOK), -1, jnp.int32)

    def tok_rows(yb, cb, p):
        return pl.ds(aligned(yb * (2 * TOK) + cb * TOK + p * PIECE, PIECE), PIECE)

    def wx_rows(xb):
        return pl.ds(aligned(xb * WBLK, WBLK), WBLK)

    blank = jnp.zeros((WBLK - 2 * ROWS, D), BF16)
    wx[wx_rows(x), :] = jnp.concatenate([w_ref[:, 0, :], w_ref[:, 1, :], blank], axis=0)
    for k in range(NX):
        scat[k * DEPTH + SLOTS_E : (k + 1) * DEPTH, :] = jnp.zeros((DEPTH - SLOTS_E, D), BF16)

    r0 = wrap(x - 2 * c, NX)
    is_owner = r0 < 2
    l_own = lax.rem(r0, 2)

    pl.semaphore_wait(barrier, len(greeted))

    sent = []

    def start(cp):
        cp.start()
        sent.append(cp)

    def y_copy(direction, hop, p):
        step = 1 if direction == UP else -1
        yb = wrap(y - step * (hop - 1), NY)
        view = tokv.at[tok_rows(yb, c, p), :]
        at = (direction, hop - 1, p)
        return copy(view, view, y_s.at[at], y_r.at[at], peer(dy=step))

    def y_arrival(direction, hop, p):
        step = 1 if direction == UP else -1
        yb = wrap(y - step * hop, NY)
        view = tokv.at[tok_rows(yb, c, p), :]
        at = (direction, hop - 1, p)
        return yb, copy(view, view, y_s.at[at], y_r.at[at], peer(dy=step))

    def to_sibling(n, p):
        yb = wrap(y + REL[n], NY)
        view = tokv.at[tok_rows(yb, c, p), :]
        start(copy(view, view, c_s.at[n, p], c_r.at[n, p], peer(dc=1)))

    def y_recv(direction, hop, p):
        _, cp = y_arrival(direction, hop, p)
        cp.wait_recv()
        if hop < 3 or (hop == 3 and p == direction):
            start(y_copy(direction, hop + 1, p))
        step = 1 if direction == UP else -1
        n = REL.index(-step * hop) if hop < 4 else 7
        to_sibling(n, p)

    def x_weights():
        for k in range(1, NX):
            view = wx.at[wx_rows(x), :]
            start(copy(view, view, w_s.at[k], w_r.at[k], peer(dx=k)))

    def x_weights_recv():
        for k in range(1, NX):
            view = wx.at[wx_rows(wrap(x - k, NX)), :]
            copy(view, view, w_s.at[k], w_r.at[k], peer(dx=k)).wait_recv()
        pick = jnp.where(
            lax.broadcasted_iota(jnp.int32, (ZBLK, NX * WBLK), 0) == lay_ref[5:6, 0 : NX * WBLK],
            1.0,
            0.0,
        ).astype(BF16)
        wst[pl.ds(aligned(z * ZBLK, 16), ZBLK), :] = dot(pick, wx[...]).astype(BF16)
        for p in range(2):
            for direction in (UP, DOWN):
                start(z_copy(direction, 1, p))

    def z_view(zb, p):
        first, count = ZPIECES[p]
        return wst.at[pl.ds(aligned(zb * ZBLK + first, 16), count), :]

    def z_copy(direction, hop, p):
        step = 1 if direction == UP else -1
        view = z_view(wrap(z - step * (hop - 1), NZ), p)
        at = (direction, hop - 1, p)
        return copy(view, view, z_s.at[at], z_r.at[at], peer(dz=step))

    def z_recv(direction, hop, p):
        step = 1 if direction == UP else -1
        view = z_view(wrap(z - step * hop, NZ), p)
        at = (direction, hop - 1, p)
        copy(view, view, z_s.at[at], z_r.at[at], peer(dz=step)).wait_recv()
        if hop < 3 or (hop == 3 and p == direction):
            start(z_copy(direction, hop + 1, p))

    def z_both(hop, p):
        z_recv(UP, hop, p)
        z_recv(DOWN, hop, p)

    def up_grad():
        def tile(t, carry):
            rows = pl.ds(aligned(t * 64, 64), 64)
            g = gate_ref[rows, :].astype(F32)
            a = adj_ref[rows, :].astype(F32)
            u_ref[rows, :] = (a * (g / (1.0 + jnp.exp(-g)))).astype(BF16)
            return carry

        lax.fori_loop(0, FF // 64, tile, 0)

    def to_owner(l, make):
        k = wrap(x - 2 * c - l, NX)

        @pl.when(k != 0)
        def _():
            make(k, ((z * NX + 2 * c + l), me)).start()

    def u_copy(l):
        def make(k, device):
            return copy(
                uown.at[l, :, pl.ds(0, 256)],
                ucat.at[:, pl.ds(aligned(k * DEPTH, DEPTH), 256)],
                uc_s.at[l, 0],
                uc_r.at[k, 0],
                device,
            )

        return make

    def u_tail_copy(l):
        def make(k, device):
            return copy(utail.at[l], utails.at[k], uc_s.at[l, 1], uc_r.at[k, 1], device)

        return make

    def unpack(k):
        lane = lax.broadcasted_iota(jnp.int32, (HALF, 128), 1)
        both = utails[k].astype(F32)
        for t in range(2):
            moved = both if t == 0 else jnp.concatenate([both[:, 64:], both[:, :64]], axis=1)
            ucat[t * HALF : (t + 1) * HALF, k * DEPTH + 256 : (k + 1) * DEPTH] = jnp.where(
                lane < 64, moved, 0.0
            ).astype(BF16)

    def s_copy(l, g):
        def make(k, device):
            return copy(
                sown.at[l, pl.ds(g * GROUP, GROUP), :],
                scat.at[pl.ds(aligned(k * DEPTH + g * GROUP, 16), GROUP), :],
                sc_s.at[l, g],
                sc_r.at[k, g],
                device,
            )

        return make

    def expert_major():
        chip = jnp.bitwise_and(lay_ref[0:1, 0:DEPTH] + y, NY - 1)
        for l in range(2):
            source = chip * (4 * CAP) + lay_ref[1:2, 0:DEPTH] + l * CAP
            pick = jnp.where(
                lax.broadcasted_iota(jnp.int32, (SLOTS, DEPTH), 0) == source, 1.0, 0.0
            ).astype(BF16)
            tails = []
            for t in range(2):
                rows = slice(t * HALF, (t + 1) * HALF)
                full = dot(u_ref[rows, :], pick)
                uown[l, rows, :] = full.astype(BF16)
                tails.append(full[:, 256 : 256 + 64])
            utail[l] = jnp.concatenate(tails, axis=1).astype(BF16)
            to_owner(l, u_copy(l))
            to_owner(l, u_tail_copy(l))

    def source_major():
        row = lax.broadcasted_iota(jnp.int32, (SLOTS, SLOTS), 0)
        col = lax.broadcasted_iota(jnp.int32, (SLOTS, SLOTS), 1)
        utj[...] = dot_nt(jnp.where(row == col, 1.0, 0.0).astype(BF16), u_ref[...]).astype(BF16)

    def stacked(t):
        cols = slice(t * 512, min((t + 1) * 512, WALL))
        width = cols.stop - cols.start
        pick = jnp.where(
            lax.broadcasted_iota(jnp.int32, (FF, width), 0) == lay_ref[3:4, cols], 1.0, 0.0
        ).astype(BF16)
        which = lay_ref[4:5, cols]
        tile = 8 * CAP
        row = lax.broadcasted_iota(jnp.int32, (tile, width), 0)
        row_expert = jnp.zeros((tile, width), jnp.int32)
        for edge in range(1, 8):
            row_expert = jnp.where(row >= edge * CAP, edge % 2, row_expert)
        keep = row_expert == which
        full = dot(utj[...], pick)
        for first in range(0, SLOTS, tile):
            rows = slice(first, first + tile)
            ustt[rows, cols] = jnp.where(keep, full[rows, :], 0.0).astype(BF16)

    def gather(g):
        chips = [wrap(y + REL[n], NY) for n in (2 * g, 2 * g + 1)]
        for n, yb in zip((2 * g, 2 * g + 1), chips):
            for p in range(2):
                view = tokv.at[tok_rows(yb, 1 - c, p), :]
                copy(view, view, c_s.at[n, p], c_r.at[n, p], peer(dc=1)).wait_recv()
        far = 1 << 12
        codes = []
        for b in range(4):
            codes.append(tbl[chips[b // 2] * 2 + b % 2] + b * far)
        codes = jnp.concatenate(codes, axis=1)
        row = lax.broadcasted_iota(jnp.int32, (GROUP, 4 * TOK), 0)
        want = row
        for b in range(1, 4):
            want = jnp.where(row >= b * CAP, row + b * (far - CAP), want)
        hits = []
        for l in range(2):
            base = want + (2 * me + l) * 32
            hit = jnp.zeros((GROUP, 4 * TOK), F32)
            for k in range(TOP):
                hit = hit + jnp.where(codes[k : k + 1, :] == base, 1.0, 0.0)
            hits.append(hit)
        pick = jnp.concatenate(hits, axis=0).astype(BF16)
        got = jnp.zeros((2 * GROUP, D), F32)
        for i in range(2):
            tokens = tokv[pl.ds(aligned(chips[i] * 2 * TOK, 2 * TOK), 2 * TOK), :]
            got = got + dot(pick[:, i * 2 * TOK : (i + 1) * 2 * TOK], tokens)
        got = got.astype(BF16)
        for l in range(2):
            sown[l, g * GROUP : (g + 1) * GROUP, :] = got[l * GROUP : (l + 1) * GROUP, :]
            to_owner(l, s_copy(l, g))

        @pl.when(is_owner)
        def _():
            scat[g * GROUP : (g + 1) * GROUP, :] = sown[l_own, g * GROUP : (g + 1) * GROUP, :]

    for i in range(1, NE):
        j = lax.rem(me + i, NE)
        start(copy(tbl.at[me], tbl.at[me], t_s.at[i], t_r.at[i], (dp, j)))
    for p in range(2):
        for direction in (UP, DOWN):
            start(y_copy(direction, 1, p))
    x_weights()
    for p in range(2):
        to_sibling(0, p)

    def y_both(hop, p):
        y_recv(UP, hop, p)
        y_recv(DOWN, hop, p)

    for cp in loads[4:]:
        cp.wait()
    up_grad()
    expert_major()
    y_both(1, 0)
    x_weights_recv()
    y_both(1, 1)
    for i in range(1, NE):
        j = lax.rem(me + NE - i, NE)
        copy(tbl.at[j], tbl.at[j], t_s.at[i], t_r.at[i], (dp, j)).wait_recv()
    gather(0)
    source_major()
    y_both(2, 0)
    stacked(0)
    z_both(1, 0)
    y_both(2, 1)
    gather(1)
    stacked(1)
    y_both(3, 0)
    z_both(1, 1)
    stacked(2)
    y_both(3, 1)
    gather(2)
    z_both(2, 0)
    y_recv(UP, 4, 0)
    y_recv(DOWN, 4, 1)
    gather(3)
    z_both(2, 1)
    z_both(3, 0)

    z2 = z // 2
    order = [wrap(z2 + k, 4) for k in (2, 1, 3, 0)]

    def cols2(i):
        return pl.ds(aligned(order[i] * 256, 256), 256)

    def z_part(i, k):
        zeta = order[i] * 2 + k
        view = zsend.at[:, pl.ds(aligned(zeta * 128, 128), 128)]
        return copy(view, zrecv.at[z], zp_s.at[i, k], zp_r.at[z], (zeta * NX + x, me))

    @pl.when(is_owner)
    def _():
        ucat[:, 0:DEPTH] = uown[l_own]
        for k in range(1, NX):
            view = ucat.at[:, pl.ds(k * DEPTH, 256)]
            copy(view, view, uc_s.at[0, 0], uc_r.at[k, 0], peer(dx=k)).wait_recv()
            view = utails.at[k]
            copy(view, view, uc_s.at[0, 1], uc_r.at[k, 1], peer(dx=k)).wait_recv()
            unpack(k)
        for g in range(4):
            for k in range(1, NX):
                view = scat.at[pl.ds(k * DEPTH + g * GROUP, GROUP), :]
                copy(view, view, sc_s.at[0, 0], sc_r.at[k, g], peer(dx=k)).wait_recv()
        for i in range(4):
            halves = []
            for t in range(2):
                rows = slice(t * HALF, (t + 1) * HALF)
                halves.append(dot(ucat[rows, :], scat[:, cols2(i)]))
                zsend[rows, cols2(i)] = halves[t].astype(BF16)
            if i < 3:
                z_part(i, 0).start()
                z_part(i, 1).start()
            else:

                @pl.when(lax.rem(z, 2) == 0)
                def _():
                    z_part(i, 1).start()
                    for t in range(2):
                        zown[t * HALF : (t + 1) * HALF, :] = halves[t][:, 0:128]

                @pl.when(lax.rem(z, 2) == 1)
                def _():
                    z_part(i, 0).start()
                    for t in range(2):
                        zown[t * HALF : (t + 1) * HALF, :] = halves[t][:, 128:256]

    def slot_grads(n):
        cols = slice(n * 256, (n + 1) * 256)
        sg[:, cols] = dot(ustt[...], wst[:, cols]).astype(BF16)

    def chip_rows(yb):
        return pl.ds(aligned(yb * GROUP, 16), GROUP)

    z_both(3, 1)
    z_recv(UP, 4, 0)
    z_recv(DOWN, 4, 1)
    for n in range(4):
        slot_grads(n)
    for k in (4, 3, 5, 2, 6, 1, 7):
        yb = wrap(y + k, NY)
        start(
            copy(
                sg.at[chip_rows(yb), :],
                ret.at[chip_rows(y), :],
                rt_s.at[k],
                rt_r.at[k],
                (dp, yb * 2 + c),
            )
        )
    ret[chip_rows(y), :] = sg[chip_rows(y), :]

    codes = jnp.concatenate([tbl[2 * y], tbl[2 * y + 1] + (1 << 12)], axis=1)
    row = lax.broadcasted_iota(jnp.int32, (GROUP, 2 * TOK), 0)
    want = row
    for b in range(1, 4):
        want = jnp.where(row >= b * CAP, row + (b // 2) * (1 << 12) + (b % 2) * 32 - b * CAP, want)
    picks = []
    for yb in range(NY):
        base = want + (yb * 4 + 2 * c) * 32
        hit = jnp.zeros((GROUP, 2 * TOK), F32)
        for k in range(TOP):
            hit = hit + jnp.where(codes[k : k + 1, :] == base, 1.0, 0.0)
        picks.append(hit)
    picked[...] = jnp.concatenate(picks, axis=0).T.astype(BF16)

    zcols = pl.ds(aligned(z * 128, 128), 128)

    def ag_view(zb, p):
        return grad.at[pl.ds(p * HALF, HALF), pl.ds(aligned(zb * 128, 128), 128)]

    def ag_copy(direction, hop, p):
        step = 1 if direction == UP else -1
        view = ag_view(wrap(z - step * (hop - 1), NZ), p)
        at = (direction, hop - 1, p)
        return copy(view, view, ag_s.at[at], ag_r.at[at], peer(dz=step))

    def ag_recv(direction, hop, p):
        step = 1 if direction == UP else -1
        view = ag_view(wrap(z - step * hop, NZ), p)
        at = (direction, hop - 1, p)
        copy(view, view, ag_s.at[at], ag_r.at[at], peer(dz=step)).wait_recv()
        if hop < 3 or (hop == 3 and p == direction):
            ag_copy(direction, hop + 1, p).start()

    def rows_copy(k):
        xd = wrap(x + k, NX)
        return copy(
            rows_ref.at[pl.ds(aligned(xd * 32, 32), 32), :],
            fin.at[l_own],
            fn_s.at[k],
            fn_r.at[l_own],
            peer(dx=k),
        )

    @pl.when(is_owner)
    def _():
        total = zown[...]
        for k in range(1, NZ):
            src = wrap(z + k, NZ)
            view = zrecv.at[src]
            copy(view, view, zp_s.at[0, 0], zp_r.at[src], peer(dz=k)).wait_recv()
            total = total + zrecv[src].astype(F32)
        grad[:, zcols] = total.astype(BF16)
        for p in range(2):
            for direction in (UP, DOWN):
                ag_copy(direction, 1, p).start()
        squares = jnp.zeros((1, 256), F32)
        for hop in range(1, 5):
            if hop < 4:
                for p in range(2):
                    for direction in (UP, DOWN):
                        ag_recv(direction, hop, p)
                pair = (z - hop, z + hop)
            else:
                ag_recv(UP, 4, 0)
                ag_recv(DOWN, 4, 1)
                pair = (z + 4, z)
            both = jnp.concatenate(
                [grad[:, pl.ds(aligned(wrap(zb, NZ) * 128, 128), 128)] for zb in pair], axis=1
            )
            wide = both.astype(F32)
            squares = squares + jnp.sum(wide * wide, axis=0, keepdims=True)
            for t in range(2):
                rows = slice(t * HALF, (t + 1) * HALF)
                term = dot_nt(both[rows, :], both)
                gram_sum[rows, :] = term if hop == 1 else gram_sum[rows, :] + term
        norm = jnp.sqrt(jnp.sum(squares, axis=1, keepdims=True))
        inverse = 1.0 / (norm + EPSILON)
        gram[...] = (gram_sum[...] * inverse * inverse).astype(BF16)

        halves = [slice(0, HALF), slice(HALF, FF)]
        for rows in halves:
            square = dot(gram[rows, :], gram[...])
            poly[rows, :] = (QUINT_B * gram[rows, :].astype(F32) + QUINT_C * square).astype(BF16)
        for rows in halves:
            x1_ref[rows, :] = (
                inverse * (QUINT_A * grad[rows, :].astype(F32) + dot(poly[rows, :], grad[...]))
            ).astype(BF16)
        for rows in halves:
            gram[rows, :] = dot_nt(x1_ref[rows, :], x1_ref[...]).astype(BF16)
        picks = []
        for xd in range(NX):
            r = lax.broadcasted_iota(jnp.int32, (32, FF), 0)
            f = lax.broadcasted_iota(jnp.int32, (32, FF), 1)
            hit = jnp.logical_and(r < ROWS, f == r + (z * NX + xd) * ROWS)
            picks.append(jnp.where(hit, 1.0, 0.0))
        pick = jnp.concatenate(picks, axis=0).astype(BF16)
        gram_rows = dot(pick, gram[...]).astype(BF16)
        it_rows = dot(pick, x1_ref[...])
        poly_rows = (QUINT_B * gram_rows.astype(F32) + QUINT_C * dot(gram_rows, gram[...])).astype(
            BF16
        )
        rows_ref[...] = (QUINT_A * it_rows + dot(poly_rows, x1_ref[...])).astype(BF16)
        for k in range(1, NX):
            rows_copy(k).start()
        fin[l_own] = rows_ref[pl.ds(aligned(x * 32, 32), 32), :]

    for k in range(1, NY):
        view = ret.at[chip_rows(wrap(y - k, NY)), :]
        copy(view, view, rt_s.at[k], rt_r.at[k], peer(dy=k)).wait_recv()

    def core_rows(core):
        return pl.ds(aligned(core * TOK, TOK), TOK)

    for_sibling[...] = dot(picked[core_rows(1 - c), :], ret[...])
    sibling = copy(for_sibling, from_sibling, sib_s, sib_r, peer(dc=1))
    start(sibling)
    mine = dot(picked[core_rows(c), :], ret[...])
    sibling.wait_recv()
    out_tok[...] = (mine + from_sibling[...]).astype(BF16)

    scale = 0.2 * math.sqrt(max(FF, D))
    for l in range(2):
        owner_x = 2 * c + l

        @pl.when(x != owner_x)
        def _():
            view = fin.at[l]
            copy(view, view, fn_s.at[1], fn_r.at[l], peer(dx=1)).wait_recv()

        out_mu[:, l, :] = scale * fin[l, 0:ROWS, :].astype(F32)

    for cp in sent:
        cp.wait_send()

    for l in range(2):
        k = wrap(x - 2 * c - l, NX)

        @pl.when(k != 0)
        def _():
            device = (z * NX + 2 * c + l, me)
            u_copy(l)(k, device).wait_send()
            u_tail_copy(l)(k, device).wait_send()
            for g in range(4):
                s_copy(l, g)(k, device).wait_send()

    @pl.when(is_owner)
    def _():
        for i in range(3):
            z_part(i, 0).wait_send()
            z_part(i, 1).wait_send()

        @pl.when(lax.rem(z, 2) == 0)
        def _():
            z_part(3, 1).wait_send()

        @pl.when(lax.rem(z, 2) == 1)
        def _():
            z_part(3, 0).wait_send()

        for hop in range(1, 5):
            for p in range(2):
                for direction in (UP, DOWN):
                    if hop < 4 or p == direction:
                        ag_copy(direction, hop, p).wait_send()
        for k in range(1, NX):
            rows_copy(k).wait_send()


def body(tokens, weights, gate, adjoint, chosen, seat, quota):
    vmem = pl.BlockSpec(memory_space=pltpu.VMEM)
    anywhere = pl.BlockSpec(memory_space=pl.ANY)
    sem = pltpu.SemaphoreType.DMA
    scratch = [
        pltpu.VMEM((ROWS, 2, D), BF16),
        pltpu.VMEM((FF, SLOTS), BF16),
        pltpu.VMEM((FF, SLOTS), BF16),
        pltpu.VMEM((TOP, TOK), jnp.int32),
        pltpu.VMEM((TOP, TOK), jnp.int32),
        pltpu.VMEM((8, WALL), jnp.int32),
        sem((7,)),
        pltpu.VMEM((NE * TOK, D), BF16),
        pltpu.VMEM((NX * WBLK, D), BF16),
        pltpu.VMEM((WALL, D), BF16),
        pltpu.VMEM((NE, 8, TOK), jnp.int32),
        pltpu.VMEM((FF, SLOTS), BF16),
        pltpu.VMEM((2, FF, DEPTH), BF16),
        pltpu.VMEM((2, HALF, 128), BF16),
        pltpu.VMEM((NX, HALF, 128), BF16),
        pltpu.VMEM((FF, NX * DEPTH), BF16),
        pltpu.VMEM((SLOTS, FF), BF16),
        pltpu.VMEM((SLOTS, WALL), BF16),
        pltpu.VMEM((2, SLOTS_E, D), BF16),
        pltpu.VMEM((NX * DEPTH, D), BF16),
        pltpu.VMEM((FF, D), BF16),
        pltpu.VMEM((FF, 128), F32),
        pltpu.VMEM((NZ, FF, 128), BF16),
        pltpu.VMEM((SLOTS, D), BF16),
        pltpu.VMEM((SLOTS, D), BF16),
        pltpu.VMEM((FF, D), BF16),
        pltpu.VMEM((FF, D), BF16),
        pltpu.VMEM((FF, FF), F32),
        pltpu.VMEM((FF, FF), BF16),
        pltpu.VMEM((FF, FF), BF16),
        pltpu.VMEM((128, D), BF16),
        pltpu.VMEM((2, 32, D), BF16),
        sem((NE,)),
        sem((NE,)),
        sem((2, 4, 2)),
        sem((2, 4, 2)),
        sem((8, 2)),
        sem((8, 2)),
        sem((NX,)),
        sem((NX,)),
        sem((2, 4, 2)),
        sem((2, 4, 2)),
        sem((2, 2)),
        sem((NX, 2)),
        sem((2, 4)),
        sem((NX, 4)),
        sem((4, 2)),
        sem((NZ,)),
        sem((2, 4, 2)),
        sem((2, 4, 2)),
        sem((NY,)),
        sem((NY,)),
        sem((NX,)),
        sem((2,)),
        pltpu.VMEM((2 * TOK, SLOTS), BF16),
        pltpu.VMEM((TOK, D), F32),
        pltpu.VMEM((TOK, D), F32),
        sem,
        sem,
    ]
    return pl.pallas_call(
        kernel,
        out_shape=(
            jax.ShapeDtypeStruct((TOK, D), BF16),
            jax.ShapeDtypeStruct((ROWS, 2, D), F32),
        ),
        in_specs=[anywhere] * 6 + [pl.BlockSpec(memory_space=pltpu.SMEM), anywhere],
        out_specs=(vmem, vmem),
        scratch_shapes=scratch,
        compiler_params=pltpu.CompilerParams(
            collective_id=0, has_side_effects=True, vmem_limit_bytes=60 * 2**20
        ),
        cost_estimate=pl.CostEstimate(
            flops=16 * 10**9, bytes_accessed=5 * 10**6, transcendentals=450560
        ),
        name="expert_backward",
    )(tokens, weights, gate, adjoint, chosen.T, seat.T, quota, jnp.asarray(layout_tables()))


def solution(mesh):
    return jax.shard_map(
        body,
        mesh=mesh,
        in_specs=(
            P(("dp", "expert"), None),
            P("dp", "expert", None),
            P(None, ("dp", "expert")),
            P(None, ("dp", "expert")),
            P(("dp", "expert"), None),
            P(("dp", "expert"), None),
            P(),
        ),
        out_specs=(P(("dp", "expert"), None), P("dp", "expert", None)),
        check_vma=False,
    )
```

time: 115 us -> 102 us (0.89)
  Pallas kernels: 110 us -> 98.4 us
  local copies, waits for them, and re-layouts: 3.62 us -> 2.38 us
    pallas_call x1, Pallas kernels: 110 us -> 98.4 us  [body(): pl.pallas_call(kernel, out_shape=(jax.ShapeDtypeStruct((TOK, D), BF16), j...]
where the time goes in v2:
time: 102 us; the launch traced here: 101 us
  Pallas kernels  98.4 us (96%)
  local copies, waits for them, and re-layouts  2.38 us (2%)
    pallas_call x1, Pallas kernels, body(): pl.pallas_call(kernel, out_shape=(jax.ShapeDtypeStruct((TOK, D), BF16), j...  98.4 us
    unnamed x4, local copies, waits for them, and re-layouts  2.38 us

profile of v2, /device:TPU:6, one launch (start us, length us, event | category | flops | bytes accessed | tf_op | source)
XLA Modules:
  0.0 101.4 jit_solution(12639168237748957388)
XLA Ops:
  0.6 98.4 %expert_backward.1 = (bf16[128,1024]{1,0:T(8,128)(2,1)}, f32[22,2,1024]{2,1,0:T(2,128)}) custom-call(bf16[128,1024]{1,0:T(8,128)(2,1)} %tok_hbm.1, bf16[22,2,1024]{2,1,0:T(2,128)(2,1)} %w_hbm.1, bf16[704,640]{1,0:T(8,128)(2,1)} %gate_hbm.1, bf16[704,640]{1,0:T(8,128)(2,1)} %adj_hbm.1, s32[6,128]{1,0:T(8,128)} %bitcast.2, s32[6,128]{1,0:T(8,128)} %bitcast.3, ...), custom_call_target="tpu_custom_call" | custom-call | flops 16000000000 | bytes 5000000 | tf_op jit(solution)/shard_map/expert_backward/pallas_call | solution.py:775
  99.0 0.0 copy-start
  99.1 1.7 %copy.12 = bf16[128,1024]{1,0:T(8,128)(2,1)} copy(bf16[128,1024]{1,0:T(8,128)(2,1)} %get-tuple-element.4) | data formatting | bytes 524288
  100.8 0.0 copy-done
  100.8 0.7 copy.13
Async XLA Ops:
  99.0 1.7 %copy-start = (f32[22,2,1024]{2,1,0:T(2,128)S(1)}, f32[22,2,1024]{2,1,0:T(2,128)}, u32[]{:S(2)}) copy-start(f32[22,2,1024]{2,1,0:T(2,128)} %get-tuple-element.5) | copy-start | bytes 540676

commit v3 on v2

--- a/solution.py
+++ b/solution.py
@@ -25,23 +25,23 @@
 CAP = 20
 SLOTS = 2 * NE * CAP
 ROWS = FF // (NX * NZ)
-WBLK = 48
+WPAD = 32
 GROUP = 4 * CAP
 SLOTS_E = NE * CAP
 DEPTH = 384
-WROWS = 2 * ROWS
-ZBLK = NX * WROWS
-WALL = NZ * ZBLK
-ZPIECES = ((0, 96), (96, ZBLK - 96))
+ZROWS = NX * ROWS
+ZBLK = 96
+ZPIECES = ((0, 48), (48, 48))
 REL = (0, -1, 1, -2, 2, -3, 3, 4)
 HALF = FF // 2
+PART = FF // 4
 PIECE = TOK // 2
 
 UP, DOWN = 0, 1
 
 
 def layout_tables():
-    table = np.full((8, WALL), -1, np.int32)
+    table = np.full((8, DEPTH), -1, np.int32)
     table[1, :] = -(1 << 20)
     for n in range(NY):
         for core in range(2):
@@ -49,18 +49,9 @@
                 at = (n * 2 + core) * CAP + p
                 table[0, at] = REL[n] % NY
                 table[1, at] = core * 2 * CAP + p
-    for j in range(NE):
-        for l in range(2):
-            for p in range(CAP):
-                table[2, (j * 2 + l) * CAP + p] = l
-    for d in range(NX * NZ):
-        for l in range(2):
-            for i in range(ROWS):
-                table[3, d * WROWS + l * ROWS + i] = d * ROWS + i
-                table[4, d * WROWS + l * ROWS + i] = l
     for k in range(NX):
-        for i in range(WROWS):
-            table[5, k * WBLK + i] = k * WROWS + i
+        for i in range(ROWS):
+            table[2, k * WPAD + i] = k * ROWS + i
     return table
 
 
@@ -91,6 +82,7 @@
     lay_ref,
     in_s,
     tokv,
+    wsend,
     wx,
     wst,
     tbl,
@@ -99,14 +91,19 @@
     utail,
     utails,
     ucat,
-    utj,
-    ustt,
+    ut,
+    wnat,
     sown,
     scat,
     zsend,
     zown,
-    zrecv,
+    near,
+    third,
+    fourth,
+    far,
     sg,
+    sgl,
+    sgo,
     ret,
     grad,
     x1_ref,
@@ -129,8 +126,16 @@
     uc_r,
     sc_s,
     sc_r,
-    zp_s,
-    zp_r,
+    sg_s,
+    sg_r,
+    nr_s,
+    nr_r,
+    th_s,
+    th_r,
+    fo_s,
+    fo_r,
+    fr_s,
+    fr_r,
     ag_s,
     ag_r,
     rt_s,
@@ -203,10 +208,11 @@
         return pl.ds(aligned(yb * (2 * TOK) + cb * TOK + p * PIECE, PIECE), PIECE)
 
     def wx_rows(xb):
-        return pl.ds(aligned(xb * WBLK, WBLK), WBLK)
-
-    blank = jnp.zeros((WBLK - 2 * ROWS, D), BF16)
-    wx[wx_rows(x), :] = jnp.concatenate([w_ref[:, 0, :], w_ref[:, 1, :], blank], axis=0)
+        return pl.ds(aligned(xb * WPAD, WPAD), WPAD)
+
+    blank = jnp.zeros((WPAD - ROWS, D), BF16)
+    for l in range(2):
+        wsend[l] = jnp.concatenate([w_ref[:, l, :], blank], axis=0)
     for k in range(NX):
         scat[k * DEPTH + SLOTS_E : (k + 1) * DEPTH, :] = jnp.zeros((DEPTH - SLOTS_E, D), BF16)
 
@@ -250,24 +256,37 @@
         n = REL.index(-step * hop) if hop < 4 else 7
         to_sibling(n, p)
 
+    def to_owner(l, make):
+        k = wrap(x - 2 * c - l, NX)
+
+        @pl.when(k != 0)
+        def _():
+            make(k, ((z * NX + 2 * c + l), me)).start()
+
+    def w_copy(l):
+        def make(k, device):
+            return copy(wsend.at[l], wx.at[wx_rows(x), :], w_s.at[l], w_r.at[k], device)
+
+        return make
+
     def x_weights():
+        for l in range(2):
+            to_owner(l, w_copy(l))
+
+    def x_weights_recv():
+        wx[wx_rows(x), :] = wsend[l_own]
         for k in range(1, NX):
-            view = wx.at[wx_rows(x), :]
-            start(copy(view, view, w_s.at[k], w_r.at[k], peer(dx=k)))
-
-    def x_weights_recv():
-        for k in range(1, NX):
-            view = wx.at[wx_rows(wrap(x - k, NX)), :]
-            copy(view, view, w_s.at[k], w_r.at[k], peer(dx=k)).wait_recv()
+            view = wx.at[wx_rows(wrap(x + k, NX)), :]
+            copy(view, view, w_s.at[0], w_r.at[k], peer(dx=k)).wait_recv()
         pick = jnp.where(
-            lax.broadcasted_iota(jnp.int32, (ZBLK, NX * WBLK), 0) == lay_ref[5:6, 0 : NX * WBLK],
+            lax.broadcasted_iota(jnp.int32, (ZBLK, NX * WPAD), 0) == lay_ref[2:3, 0 : NX * WPAD],
             1.0,
             0.0,
         ).astype(BF16)
         wst[pl.ds(aligned(z * ZBLK, 16), ZBLK), :] = dot(pick, wx[...]).astype(BF16)
         for p in range(2):
             for direction in (UP, DOWN):
-                start(z_copy(direction, 1, p))
+                z_copy(direction, 1, p).start()
 
     def z_view(zb, p):
         first, count = ZPIECES[p]
@@ -285,7 +304,7 @@
         at = (direction, hop - 1, p)
         copy(view, view, z_s.at[at], z_r.at[at], peer(dz=step)).wait_recv()
         if hop < 3 or (hop == 3 and p == direction):
-            start(z_copy(direction, hop + 1, p))
+            z_copy(direction, hop + 1, p).start()
 
     def z_both(hop, p):
         z_recv(UP, hop, p)
@@ -300,13 +319,6 @@
             return carry
 
         lax.fori_loop(0, FF // 64, tile, 0)
-
-    def to_owner(l, make):
-        k = wrap(x - 2 * c - l, NX)
-
-        @pl.when(k != 0)
-        def _():
-            make(k, ((z * NX + 2 * c + l), me)).start()
 
     def u_copy(l):
         def make(k, device):
@@ -364,28 +376,38 @@
             to_owner(l, u_copy(l))
             to_owner(l, u_tail_copy(l))
 
-    def source_major():
-        row = lax.broadcasted_iota(jnp.int32, (SLOTS, SLOTS), 0)
-        col = lax.broadcasted_iota(jnp.int32, (SLOTS, SLOTS), 1)
-        utj[...] = dot_nt(jnp.where(row == col, 1.0, 0.0).astype(BF16), u_ref[...]).astype(BF16)
-
-    def stacked(t):
-        cols = slice(t * 512, min((t + 1) * 512, WALL))
-        width = cols.stop - cols.start
-        pick = jnp.where(
-            lax.broadcasted_iota(jnp.int32, (FF, width), 0) == lay_ref[3:4, cols], 1.0, 0.0
+    def u_recv():
+        ucat[:, 0:DEPTH] = uown[l_own]
+        for k in range(1, NX):
+            view = ucat.at[:, pl.ds(k * DEPTH, 256)]
+            copy(view, view, uc_s.at[0, 0], uc_r.at[k, 0], peer(dx=k)).wait_recv()
+            view = utails.at[k]
+            copy(view, view, uc_s.at[0, 1], uc_r.at[k, 1], peer(dx=k)).wait_recv()
+            unpack(k)
+
+    def transposed(k):
+        row = lax.broadcasted_iota(jnp.int32, (SLOTS_E, DEPTH), 0)
+        col = lax.broadcasted_iota(jnp.int32, (SLOTS_E, DEPTH), 1)
+        same = jnp.where(row == col, 1.0, 0.0).astype(BF16)
+        ut[k * SLOTS_E : (k + 1) * SLOTS_E, :] = dot_nt(
+            same, ucat[:, k * DEPTH : (k + 1) * DEPTH]
         ).astype(BF16)
-        which = lay_ref[4:5, cols]
-        tile = 8 * CAP
-        row = lax.broadcasted_iota(jnp.int32, (tile, width), 0)
-        row_expert = jnp.zeros((tile, width), jnp.int32)
-        for edge in range(1, 8):
-            row_expert = jnp.where(row >= edge * CAP, edge % 2, row_expert)
-        keep = row_expert == which
-        full = dot(utj[...], pick)
-        for first in range(0, SLOTS, tile):
-            rows = slice(first, first + tile)
-            ustt[rows, cols] = jnp.where(keep, full[rows, :], 0.0).astype(BF16)
+
+    def slot_grads():
+        for zb in range(NZ):
+            wnat[zb * ZROWS : (zb + 1) * ZROWS, :] = wst[zb * ZBLK : zb * ZBLK + ZROWS, :]
+        for n in range(4):
+            cols = slice(n * 256, (n + 1) * 256)
+            sg[:, cols] = dot(ut[...], wnat[:, cols]).astype(BF16)
+
+    def sg_copy(k, g):
+        return copy(
+            sg.at[pl.ds(k * SLOTS_E + g * GROUP, GROUP), :],
+            sgl.at[l_own, pl.ds(g * GROUP, GROUP), :],
+            sg_s.at[k, g],
+            sg_r.at[l_own, g],
+            peer(dx=k),
+        )
 
     def gather(g):
         chips = [wrap(y + REL[n], NY) for n in (2 * g, 2 * g + 1)]
@@ -423,13 +445,13 @@
         def _():
             scat[g * GROUP : (g + 1) * GROUP, :] = sown[l_own, g * GROUP : (g + 1) * GROUP, :]
 
-    for i in range(1, NE):
-        j = lax.rem(me + i, NE)
-        start(copy(tbl.at[me], tbl.at[me], t_s.at[i], t_r.at[i], (dp, j)))
     for p in range(2):
         for direction in (UP, DOWN):
             start(y_copy(direction, 1, p))
     x_weights()
+    for i in range(1, NE):
+        j = lax.rem(me + i, NE)
+        start(copy(tbl.at[me], tbl.at[me], t_s.at[i], t_r.at[i], (dp, j)))
     for p in range(2):
         to_sibling(0, p)
 
@@ -442,51 +464,110 @@
     up_grad()
     expert_major()
     y_both(1, 0)
-    x_weights_recv()
+
+    @pl.when(is_owner)
+    def _():
+        x_weights_recv()
+
     y_both(1, 1)
     for i in range(1, NE):
         j = lax.rem(me + NE - i, NE)
         copy(tbl.at[j], tbl.at[j], t_s.at[i], t_r.at[i], (dp, j)).wait_recv()
     gather(0)
-    source_major()
+
+    @pl.when(is_owner)
+    def _():
+        z_both(1, 0)
+        z_both(1, 1)
+
     y_both(2, 0)
-    stacked(0)
-    z_both(1, 0)
+
+    @pl.when(is_owner)
+    def _():
+        z_both(2, 0)
+        z_both(2, 1)
+
     y_both(2, 1)
     gather(1)
-    stacked(1)
+
+    @pl.when(is_owner)
+    def _():
+        z_both(3, 0)
+        z_both(3, 1)
+
     y_both(3, 0)
-    z_both(1, 1)
-    stacked(2)
+
+    @pl.when(is_owner)
+    def _():
+        u_recv()
+        transposed(0)
+        transposed(1)
+
     y_both(3, 1)
     gather(2)
-    z_both(2, 0)
+
+    @pl.when(is_owner)
+    def _():
+        transposed(2)
+        transposed(3)
+        z_recv(UP, 4, 0)
+        z_recv(DOWN, 4, 1)
+
     y_recv(UP, 4, 0)
     y_recv(DOWN, 4, 1)
     gather(3)
-    z_both(2, 1)
-    z_both(3, 0)
+
+    @pl.when(is_owner)
+    def _():
+        slot_grads()
+        for g in (3, 2, 1, 0):
+            for k in range(1, NX):
+                sg_copy(k, g).start()
+        sgl[l_own] = sg[0:SLOTS_E, :]
 
     z2 = z // 2
-    order = [wrap(z2 + k, 4) for k in (2, 1, 3, 0)]
+    odd = lax.rem(z, 2)
+    order = [wrap(z2 + k, 4) for k in (2, 1 + 2 * odd, 3 - 2 * odd, 0)]
 
     def cols2(i):
         return pl.ds(aligned(order[i] * 256, 256), 256)
 
-    def z_part(i, k):
-        zeta = order[i] * 2 + k
-        view = zsend.at[:, pl.ds(aligned(zeta * 128, 128), 128)]
-        return copy(view, zrecv.at[z], zp_s.at[i, k], zp_r.at[z], (zeta * NX + x, me))
-
-    @pl.when(is_owner)
-    def _():
-        ucat[:, 0:DEPTH] = uown[l_own]
-        for k in range(1, NX):
-            view = ucat.at[:, pl.ds(k * DEPTH, 256)]
-            copy(view, view, uc_s.at[0, 0], uc_r.at[k, 0], peer(dx=k)).wait_recv()
-            view = utails.at[k]
-            copy(view, view, uc_s.at[0, 1], uc_r.at[k, 1], peer(dx=k)).wait_recv()
-            unpack(k)
+    def zchunk(r):
+        return pl.ds(aligned(wrap(z + r, NZ) * 128, 128), 128)
+
+    def direct_copy(d):
+        r, step = ((1, 1), (7, -1))[d]
+        return copy(zsend.at[:, zchunk(r)], near.at[d], nr_s.at[d], nr_r.at[d], peer(dz=step))
+
+    def third_copy(d):
+        r, step = ((3, 1), (5, -1))[d]
+        return copy(zsend.at[:, zchunk(r)], third.at[d], th_s.at[d], th_r.at[d], peer(dz=step))
+
+    def fourth_copy(d):
+        step = (2, -2)[d]
+        rows = pl.ds(d * HALF, HALF)
+        return copy(
+            zsend.at[rows, zchunk(4)], fourth.at[d], fo_s.at[d], fo_r.at[d], peer(dz=step)
+        )
+
+    def relayed_copy(d):
+        r, step = ((2, 2), (6, -2))[d]
+        return copy(zsend.at[:, zchunk(r)], far.at[d], fr_s.at[d], fr_r.at[d], peer(dz=step))
+
+    def relay(d):
+        r = (2, 6)[d]
+        third_copy(d).wait_recv()
+        fourth_copy(d).wait_recv()
+        for t in range(2):
+            rows = slice(t * HALF, (t + 1) * HALF)
+            total = zsend[rows, zchunk(r)].astype(F32) + third[d, rows, :].astype(F32)
+            if t == d:
+                total = total + fourth[d].astype(F32)
+            zsend[rows, zchunk(r)] = total.astype(BF16)
+        relayed_copy(d).start()
+
+    @pl.when(is_owner)
+    def _():
         for g in range(4):
             for k in range(1, NX):
                 view = scat.at[pl.ds(k * DEPTH + g * GROUP, GROUP), :]
@@ -497,53 +578,69 @@
                 rows = slice(t * HALF, (t + 1) * HALF)
                 halves.append(dot(ucat[rows, :], scat[:, cols2(i)]))
                 zsend[rows, cols2(i)] = halves[t].astype(BF16)
-            if i < 3:
-                z_part(i, 0).start()
-                z_part(i, 1).start()
-            else:
-
-                @pl.when(lax.rem(z, 2) == 0)
+            for parity in range(2):
+
+                @pl.when(odd == parity)
                 def _():
-                    z_part(i, 1).start()
-                    for t in range(2):
-                        zown[t * HALF : (t + 1) * HALF, :] = halves[t][:, 0:128]
-
-                @pl.when(lax.rem(z, 2) == 1)
-                def _():
-                    z_part(i, 0).start()
-                    for t in range(2):
-                        zown[t * HALF : (t + 1) * HALF, :] = halves[t][:, 128:256]
-
-    def slot_grads(n):
-        cols = slice(n * 256, (n + 1) * 256)
-        sg[:, cols] = dot(ustt[...], wst[:, cols]).astype(BF16)
+                    if i == 0:
+                        fourth_copy(0).start()
+                        fourth_copy(1).start()
+                        third_copy(1 - parity).start()
+                    elif i == 1:
+                        third_copy(parity).start()
+                    elif i == 2:
+                        direct_copy(1 - parity).start()
+                    else:
+                        direct_copy(parity).start()
+                        first = parity * 128
+                        for t in range(2):
+                            rows = slice(t * HALF, (t + 1) * HALF)
+                            zown[rows, :] = halves[t][:, first : first + 128]
 
     def chip_rows(yb):
         return pl.ds(aligned(yb * GROUP, 16), GROUP)
 
-    z_both(3, 1)
-    z_recv(UP, 4, 0)
-    z_recv(DOWN, 4, 1)
-    for n in range(4):
-        slot_grads(n)
-    for k in (4, 3, 5, 2, 6, 1, 7):
-        yb = wrap(y + k, NY)
-        start(
-            copy(
-                sg.at[chip_rows(yb), :],
-                ret.at[chip_rows(y), :],
-                rt_s.at[k],
-                rt_r.at[k],
-                (dp, yb * 2 + c),
-            )
+    def return_copy(n):
+        yb = wrap(y + REL[n], NY)
+        return copy(
+            sgo.at[pl.ds(n * GROUP, GROUP), :],
+            ret.at[chip_rows(y), :],
+            rt_s.at[n],
+            rt_r.at[n],
+            (dp, yb * 2 + c),
         )
-    ret[chip_rows(y), :] = sg[chip_rows(y), :]
+
+    def send_back(g):
+        for l in range(2):
+
+            @pl.when(x != 2 * c + l)
+            def _():
+                view = sgl.at[l, pl.ds(g * GROUP, GROUP), :]
+                copy(view, view, sg_s.at[1, g], sg_r.at[l, g], peer(dx=1)).wait_recv()
+
+        for n in (2 * g + 1, 2 * g):
+            both = [sgl[l, n * 2 * CAP : (n + 1) * 2 * CAP, :] for l in range(2)]
+            sgo[n * GROUP : (n + 1) * GROUP, :] = jnp.concatenate(both, axis=0)
+            if n:
+                start(return_copy(n))
+
+    send_back(3)
+    send_back(2)
+
+    @pl.when(is_owner)
+    def _():
+        relay(0)
+        relay(1)
+
+    send_back(1)
+    send_back(0)
+    ret[chip_rows(y), :] = sgo[0:GROUP, :]
 
     codes = jnp.concatenate([tbl[2 * y], tbl[2 * y + 1] + (1 << 12)], axis=1)
     row = lax.broadcasted_iota(jnp.int32, (GROUP, 2 * TOK), 0)
     want = row
     for b in range(1, 4):
-        want = jnp.where(row >= b * CAP, row + (b // 2) * (1 << 12) + (b % 2) * 32 - b * CAP, want)
+        want = jnp.where(row >= b * CAP, row + (b % 2) * (1 << 12) + (b // 2) * 32 - b * CAP, want)
     picks = []
     for yb in range(NY):
         base = want + (yb * 4 + 2 * c) * 32
@@ -556,7 +653,7 @@
     zcols = pl.ds(aligned(z * 128, 128), 128)
 
     def ag_view(zb, p):
-        return grad.at[pl.ds(p * HALF, HALF), pl.ds(aligned(zb * 128, 128), 128)]
+        return grad.at[pl.ds(p * PART, PART), pl.ds(aligned(zb * 128, 128), 128)]
 
     def ag_copy(direction, hop, p):
         step = 1 if direction == UP else -1
@@ -569,7 +666,7 @@
         view = ag_view(wrap(z - step * hop, NZ), p)
         at = (direction, hop - 1, p)
         copy(view, view, ag_s.at[at], ag_r.at[at], peer(dz=step)).wait_recv()
-        if hop < 3 or (hop == 3 and p == direction):
+        if hop < 3 or (hop == 3 and p // 2 == direction):
             ag_copy(direction, hop + 1, p).start()
 
     def rows_copy(k):
@@ -585,25 +682,27 @@
     @pl.when(is_owner)
     def _():
         total = zown[...]
-        for k in range(1, NZ):
-            src = wrap(z + k, NZ)
-            view = zrecv.at[src]
-            copy(view, view, zp_s.at[0, 0], zp_r.at[src], peer(dz=k)).wait_recv()
-            total = total + zrecv[src].astype(F32)
+        for d in range(2):
+            direct_copy(d).wait_recv()
+            total = total + near[d].astype(F32)
+        for d in range(2):
+            relayed_copy(d).wait_recv()
+            total = total + far[d].astype(F32)
         grad[:, zcols] = total.astype(BF16)
-        for p in range(2):
+        for p in range(4):
             for direction in (UP, DOWN):
                 ag_copy(direction, 1, p).start()
         squares = jnp.zeros((1, 256), F32)
         for hop in range(1, 5):
             if hop < 4:
-                for p in range(2):
+                for p in range(4):
                     for direction in (UP, DOWN):
                         ag_recv(direction, hop, p)
                 pair = (z - hop, z + hop)
             else:
-                ag_recv(UP, 4, 0)
-                ag_recv(DOWN, 4, 1)
+                for p in range(2):
+                    ag_recv(UP, 4, p)
+                    ag_recv(DOWN, 4, 2 + p)
                 pair = (z + 4, z)
             both = jnp.concatenate(
                 [grad[:, pl.ds(aligned(wrap(zb, NZ) * 128, 128), 128)] for zb in pair], axis=1
@@ -645,9 +744,9 @@
             rows_copy(k).start()
         fin[l_own] = rows_ref[pl.ds(aligned(x * 32, 32), 32), :]
 
-    for k in range(1, NY):
-        view = ret.at[chip_rows(wrap(y - k, NY)), :]
-        copy(view, view, rt_s.at[k], rt_r.at[k], peer(dy=k)).wait_recv()
+    for n in range(1, NY):
+        view = ret.at[chip_rows(wrap(y - REL[n], NY)), :]
+        copy(view, view, rt_s.at[n], rt_r.at[n], peer(dy=-REL[n])).wait_recv()
 
     def core_rows(core):
         return pl.ds(aligned(core * TOK, TOK), TOK)
@@ -679,6 +778,7 @@
         @pl.when(k != 0)
         def _():
             device = (z * NX + 2 * c + l, me)
+            w_copy(l)(k, device).wait_send()
             u_copy(l)(k, device).wait_send()
             u_tail_copy(l)(k, device).wait_send()
             for g in range(4):
@@ -686,23 +786,24 @@
 
     @pl.when(is_owner)
     def _():
-        for i in range(3):
-            z_part(i, 0).wait_send()
-            z_part(i, 1).wait_send()
-
-        @pl.when(lax.rem(z, 2) == 0)
-        def _():
-            z_part(3, 1).wait_send()
-
-        @pl.when(lax.rem(z, 2) == 1)
-        def _():
-            z_part(3, 0).wait_send()
+        for d in range(2):
+            direct_copy(d).wait_send()
+            third_copy(d).wait_send()
+            fourth_copy(d).wait_send()
+            relayed_copy(d).wait_send()
 
         for hop in range(1, 5):
             for p in range(2):
                 for direction in (UP, DOWN):
                     if hop < 4 or p == direction:
+                        z_copy(direction, hop, p).wait_send()
+            for p in range(4):
+                for direction in (UP, DOWN):
+                    if hop < 4 or p // 2 == direction:
                         ag_copy(direction, hop, p).wait_send()
+        for g in range(4):
+            for k in range(1, NX):
+                sg_copy(k, g).wait_send()
         for k in range(1, NX):
             rows_copy(k).wait_send()
 
@@ -717,24 +818,30 @@
         pltpu.VMEM((FF, SLOTS), BF16),
         pltpu.VMEM((TOP, TOK), jnp.int32),
         pltpu.VMEM((TOP, TOK), jnp.int32),
-        pltpu.VMEM((8, WALL), jnp.int32),
+        pltpu.VMEM((8, DEPTH), jnp.int32),
         sem((7,)),
         pltpu.VMEM((NE * TOK, D), BF16),
-        pltpu.VMEM((NX * WBLK, D), BF16),
-        pltpu.VMEM((WALL, D), BF16),
+        pltpu.VMEM((2, WPAD, D), BF16),
+        pltpu.VMEM((NX * WPAD, D), BF16),
+        pltpu.VMEM((NZ * ZBLK, D), BF16),
         pltpu.VMEM((NE, 8, TOK), jnp.int32),
         pltpu.VMEM((FF, SLOTS), BF16),
         pltpu.VMEM((2, FF, DEPTH), BF16),
         pltpu.VMEM((2, HALF, 128), BF16),
         pltpu.VMEM((NX, HALF, 128), BF16),
         pltpu.VMEM((FF, NX * DEPTH), BF16),
-        pltpu.VMEM((SLOTS, FF), BF16),
-        pltpu.VMEM((SLOTS, WALL), BF16),
+        pltpu.VMEM((NX * SLOTS_E, FF), BF16),
+        pltpu.VMEM((FF, D), BF16),
         pltpu.VMEM((2, SLOTS_E, D), BF16),
         pltpu.VMEM((NX * DEPTH, D), BF16),
         pltpu.VMEM((FF, D), BF16),
         pltpu.VMEM((FF, 128), F32),
-        pltpu.VMEM((NZ, FF, 128), BF16),
+        pltpu.VMEM((2, FF, 128), BF16),
+        pltpu.VMEM((2, FF, 128), BF16),
+        pltpu.VMEM((2, HALF, 128), BF16),
+        pltpu.VMEM((2, FF, 128), BF16),
+        pltpu.VMEM((NX * SLOTS_E, D), BF16),
+        pltpu.VMEM((2, SLOTS_E, D), BF16),
         pltpu.VMEM((SLOTS, D), BF16),
         pltpu.VMEM((SLOTS, D), BF16),
         pltpu.VMEM((FF, D), BF16),
@@ -750,7 +857,7 @@
         sem((2, 4, 2)),
         sem((8, 2)),
         sem((8, 2)),
-        sem((NX,)),
+        sem((2,)),
         sem((NX,)),
         sem((2, 4, 2)),
         sem((2, 4, 2)),
@@ -758,10 +865,18 @@
         sem((NX, 2)),
         sem((2, 4)),
         sem((NX, 4)),
-        sem((4, 2)),
-        sem((NZ,)),
-        sem((2, 4, 2)),
-        sem((2, 4, 2)),
+        sem((NX, 4)),
+        sem((2, 4)),
+        sem((2,)),
+        sem((2,)),
+        sem((2,)),
+        sem((2,)),
+        sem((2,)),
+        sem((2,)),
+        sem((2,)),
+        sem((2,)),
+        sem((2, 4, 4)),
+        sem((2, 4, 4)),
         sem((NY,)),
         sem((NY,)),
         sem((NX,)),

time: 102 us -> 95.2 us (0.933)
  Pallas kernels: 98.4 us -> 90.8 us
    pallas_call x1, Pallas kernels: 98.4 us -> 90.8 us  [body(): pl.pallas_call(kernel, out_shape=(jax.ShapeDtypeStruct((TOK, D), BF16), j...]
where the time goes in v3:
time: 95.2 us; the launch traced here: 93.9 us
  Pallas kernels  90.8 us (95%)
  local copies, waits for them, and re-layouts  2.38 us (2%)
    pallas_call x1, Pallas kernels, body(): pl.pallas_call(kernel, out_shape=(jax.ShapeDtypeStruct((TOK, D), BF16), j...  90.8 us
    unnamed x4, local copies, waits for them, and re-layouts  2.38 us

profile of v3, /device:TPU:6, one launch (start us, length us, event | category | flops | bytes accessed | tf_op | source)
XLA Modules:
  0.0 93.9 jit_solution(11573610202627487685)
XLA Ops:
  0.6 90.8 %expert_backward.1 = (bf16[128,1024]{1,0:T(8,128)(2,1)}, f32[22,2,1024]{2,1,0:T(2,128)}) custom-call(bf16[128,1024]{1,0:T(8,128)(2,1)} %tok_hbm.1, bf16[22,2,1024]{2,1,0:T(2,128)(2,1)} %w_hbm.1, bf16[704,640]{1,0:T(8,128)(2,1)} %gate_hbm.1, bf16[704,640]{1,0:T(8,128)(2,1)} %adj_hbm.1, s32[6,128]{1,0:T(8,128)} %bitcast.2, s32[6,128]{1,0:T(8,128)} %bitcast.3, ...), custom_call_target="tpu_custom_call" | custom-call | flops 16000000000 | bytes 5000000 | tf_op jit(solution)/shard_map/expert_backward/pallas_call | solution.py:890
  91.5 0.0 copy-start
  91.5 1.7 %copy.12 = bf16[128,1024]{1,0:T(8,128)(2,1)} copy(bf16[128,1024]{1,0:T(8,128)(2,1)} %get-tuple-element.4) | data formatting | bytes 524288
  93.2 0.0 copy-done
  93.2 0.7 copy.13
Async XLA Ops:
  91.5 1.7 %copy-start = (f32[22,2,1024]{2,1,0:T(2,128)S(1)}, f32[22,2,1024]{2,1,0:T(2,128)}, u32[]{:S(2)}) copy-start(f32[22,2,1024]{2,1,0:T(2,128)} %get-tuple-element.5) | copy-start | bytes 540676

commit v4 on v3

--- a/solution.py
+++ b/solution.py
@@ -28,6 +28,7 @@
 WPAD = 32
 GROUP = 4 * CAP
 SLOTS_E = NE * CAP
+S_PARTS = ((0, 80), (80, 80), (160, 80), (240, 32), (272, 48))
 DEPTH = 384
 ZROWS = NX * ROWS
 ZBLK = 96
@@ -73,7 +74,7 @@
     quota_ref,
     lay_hbm,
     out_tok,
-    out_mu,
+    out_rows,
     w_ref,
     gate_ref,
     adj_ref,
@@ -175,7 +176,7 @@
 
     barrier = pltpu.get_barrier_semaphore()
     greeted = [(dp, lax.rem(me + i, NE)) for i in range(1, NE)]
-    greeted += [peer(dz=k) for k in range(1, NZ)]
+    greeted += [peer(dz=k) for k in (-2, -1, 1, 2)]
     greeted += [peer(dx=k) for k in range(1, NX)]
     for device in greeted:
         pl.semaphore_signal(barrier, inc=1, device_id=device, device_id_type=MESH)
@@ -228,6 +229,11 @@
         cp.start()
         sent.append(cp)
 
+    def drain():
+        for cp in sent:
+            cp.wait_send()
+        sent.clear()
+
     def y_copy(direction, hop, p):
         step = 1 if direction == UP else -1
         yb = wrap(y - step * (hop - 1), NY)
@@ -310,23 +316,25 @@
         z_recv(UP, hop, p)
         z_recv(DOWN, hop, p)
 
-    def up_grad():
-        def tile(t, carry):
-            rows = pl.ds(aligned(t * 64, 64), 64)
+    def up_grad(t):
+        def tile(i, carry):
+            rows = pl.ds(aligned(t * HALF + i * 32, 32), 32)
             g = gate_ref[rows, :].astype(F32)
             a = adj_ref[rows, :].astype(F32)
             u_ref[rows, :] = (a * (g / (1.0 + jnp.exp(-g)))).astype(BF16)
             return carry
 
-        lax.fori_loop(0, FF // 64, tile, 0)
-
-    def u_copy(l):
+        lax.fori_loop(0, HALF // 32, tile, 0)
+
+    def u_copy(l, t):
+        rows = pl.ds(t * HALF, HALF)
+
         def make(k, device):
             return copy(
-                uown.at[l, :, pl.ds(0, 256)],
-                ucat.at[:, pl.ds(aligned(k * DEPTH, DEPTH), 256)],
-                uc_s.at[l, 0],
-                uc_r.at[k, 0],
+                uown.at[l, rows, pl.ds(0, 256)],
+                ucat.at[rows, pl.ds(aligned(k * DEPTH, DEPTH), 256)],
+                uc_s.at[l, t],
+                uc_r.at[k, t],
                 device,
             )
 
@@ -334,7 +342,7 @@
 
     def u_tail_copy(l):
         def make(k, device):
-            return copy(utail.at[l], utails.at[k], uc_s.at[l, 1], uc_r.at[k, 1], device)
+            return copy(utail.at[l], utails.at[k], uc_s.at[l, 2], uc_r.at[k, 2], device)
 
         return make
 
@@ -348,10 +356,12 @@
             ).astype(BF16)
 
     def s_copy(l, g):
+        first, count = S_PARTS[g]
+
         def make(k, device):
             return copy(
-                sown.at[l, pl.ds(g * GROUP, GROUP), :],
-                scat.at[pl.ds(aligned(k * DEPTH + g * GROUP, 16), GROUP), :],
+                sown.at[l, pl.ds(first, count), :],
+                scat.at[pl.ds(aligned(k * DEPTH + first, 16), count), :],
                 sc_s.at[l, g],
                 sc_r.at[k, g],
                 device,
@@ -361,28 +371,31 @@
 
     def expert_major():
         chip = jnp.bitwise_and(lay_ref[0:1, 0:DEPTH] + y, NY - 1)
-        for l in range(2):
-            source = chip * (4 * CAP) + lay_ref[1:2, 0:DEPTH] + l * CAP
-            pick = jnp.where(
-                lax.broadcasted_iota(jnp.int32, (SLOTS, DEPTH), 0) == source, 1.0, 0.0
-            ).astype(BF16)
-            tails = []
-            for t in range(2):
-                rows = slice(t * HALF, (t + 1) * HALF)
+        tails = [[], []]
+        for t in range(2):
+            rows = slice(t * HALF, (t + 1) * HALF)
+            up_grad(t)
+            for l in range(2):
+                source = chip * (4 * CAP) + lay_ref[1:2, 0:DEPTH] + l * CAP
+                pick = jnp.where(
+                    lax.broadcasted_iota(jnp.int32, (SLOTS, DEPTH), 0) == source, 1.0, 0.0
+                ).astype(BF16)
                 full = dot(u_ref[rows, :], pick)
                 uown[l, rows, :] = full.astype(BF16)
-                tails.append(full[:, 256 : 256 + 64])
-            utail[l] = jnp.concatenate(tails, axis=1).astype(BF16)
-            to_owner(l, u_copy(l))
+                tails[l].append(full[:, 256 : 256 + 64])
+                to_owner(l, u_copy(l, t))
+        for l in range(2):
+            utail[l] = jnp.concatenate(tails[l], axis=1).astype(BF16)
             to_owner(l, u_tail_copy(l))
 
     def u_recv():
         ucat[:, 0:DEPTH] = uown[l_own]
         for k in range(1, NX):
-            view = ucat.at[:, pl.ds(k * DEPTH, 256)]
-            copy(view, view, uc_s.at[0, 0], uc_r.at[k, 0], peer(dx=k)).wait_recv()
+            for t in range(2):
+                view = ucat.at[pl.ds(t * HALF, HALF), pl.ds(k * DEPTH, 256)]
+                copy(view, view, uc_s.at[0, t], uc_r.at[k, t], peer(dx=k)).wait_recv()
             view = utails.at[k]
-            copy(view, view, uc_s.at[0, 1], uc_r.at[k, 1], peer(dx=k)).wait_recv()
+            copy(view, view, uc_s.at[0, 2], uc_r.at[k, 2], peer(dx=k)).wait_recv()
             unpack(k)
 
     def transposed(k):
@@ -409,41 +422,39 @@
             peer(dx=k),
         )
 
-    def gather(g):
-        chips = [wrap(y + REL[n], NY) for n in (2 * g, 2 * g + 1)]
-        for n, yb in zip((2 * g, 2 * g + 1), chips):
-            for p in range(2):
-                view = tokv.at[tok_rows(yb, 1 - c, p), :]
-                copy(view, view, c_s.at[n, p], c_r.at[n, p], peer(dc=1)).wait_recv()
+    def gather_chip(n):
+        yb = wrap(y + REL[n], NY)
+        for p in range(2):
+            view = tokv.at[tok_rows(yb, 1 - c, p), :]
+            copy(view, view, c_s.at[n, p], c_r.at[n, p], peer(dc=1)).wait_recv()
         far = 1 << 12
-        codes = []
-        for b in range(4):
-            codes.append(tbl[chips[b // 2] * 2 + b % 2] + b * far)
-        codes = jnp.concatenate(codes, axis=1)
-        row = lax.broadcasted_iota(jnp.int32, (GROUP, 4 * TOK), 0)
+        codes = jnp.concatenate([tbl[yb * 2], tbl[yb * 2 + 1] + far], axis=1)
+        row = lax.broadcasted_iota(jnp.int32, (GROUP, 2 * TOK), 0)
         want = row
         for b in range(1, 4):
-            want = jnp.where(row >= b * CAP, row + b * (far - CAP), want)
-        hits = []
+            want = jnp.where(row >= b * CAP, row + (b % 2) * far + (b // 2) * 32 - b * CAP, want)
+        want = want + (2 * me) * 32
+        hit = jnp.zeros((GROUP, 2 * TOK), F32)
+        for k in range(TOP):
+            hit = hit + jnp.where(codes[k : k + 1, :] == want, 1.0, 0.0)
+        tokens = tokv[pl.ds(aligned(yb * 2 * TOK, 2 * TOK), 2 * TOK), :]
+        return dot(hit.astype(BF16), tokens)
+
+    def place(g, values):
+        first, count = S_PARTS[g]
+        rows = slice(first, first + count)
         for l in range(2):
-            base = want + (2 * me + l) * 32
-            hit = jnp.zeros((GROUP, 4 * TOK), F32)
-            for k in range(TOP):
-                hit = hit + jnp.where(codes[k : k + 1, :] == base, 1.0, 0.0)
-            hits.append(hit)
-        pick = jnp.concatenate(hits, axis=0).astype(BF16)
-        got = jnp.zeros((2 * GROUP, D), F32)
-        for i in range(2):
-            tokens = tokv[pl.ds(aligned(chips[i] * 2 * TOK, 2 * TOK), 2 * TOK), :]
-            got = got + dot(pick[:, i * 2 * TOK : (i + 1) * 2 * TOK], tokens)
-        got = got.astype(BF16)
-        for l in range(2):
-            sown[l, g * GROUP : (g + 1) * GROUP, :] = got[l * GROUP : (l + 1) * GROUP, :]
+            sown[l, rows, :] = values[l].astype(BF16)
             to_owner(l, s_copy(l, g))
 
         @pl.when(is_owner)
         def _():
-            scat[g * GROUP : (g + 1) * GROUP, :] = sown[l_own, g * GROUP : (g + 1) * GROUP, :]
+            scat[rows, :] = sown[l_own, rows, :]
+
+    def gather(g):
+        two = [gather_chip(n) for n in (2 * g, 2 * g + 1)]
+        per = 2 * CAP
+        place(g, [jnp.concatenate([v[l * per : (l + 1) * per] for v in two]) for l in range(2)])
 
     for p in range(2):
         for direction in (UP, DOWN):
@@ -461,7 +472,6 @@
 
     for cp in loads[4:]:
         cp.wait()
-    up_grad()
     expert_major()
     y_both(1, 0)
 
@@ -505,6 +515,8 @@
 
     y_both(3, 1)
     gather(2)
+    sixth = gather_chip(6)
+    place(3, [sixth[0:32], sixth[40:72]])
 
     @pl.when(is_owner)
     def _():
@@ -515,7 +527,8 @@
 
     y_recv(UP, 4, 0)
     y_recv(DOWN, 4, 1)
-    gather(3)
+    seventh = gather_chip(7)
+    place(4, [jnp.concatenate([sixth[32:40], seventh[0:40]]), jnp.concatenate([sixth[72:80], seventh[40:80]])])
 
     @pl.when(is_owner)
     def _():
@@ -568,9 +581,9 @@
 
     @pl.when(is_owner)
     def _():
-        for g in range(4):
+        for g in range(5):
             for k in range(1, NX):
-                view = scat.at[pl.ds(k * DEPTH + g * GROUP, GROUP), :]
+                view = scat.at[pl.ds(k * DEPTH + S_PARTS[g][0], S_PARTS[g][1]), :]
                 copy(view, view, sc_s.at[0, 0], sc_r.at[k, g], peer(dx=k)).wait_recv()
         for i in range(4):
             halves = []
@@ -624,6 +637,21 @@
             if n:
                 start(return_copy(n))
 
+
+    drain()
+    for l in range(2):
+        k = wrap(x - 2 * c - l, NX)
+
+        @pl.when(k != 0)
+        def _():
+            device = (z * NX + 2 * c + l, me)
+            w_copy(l)(k, device).wait_send()
+            u_copy(l, 0)(k, device).wait_send()
+            u_copy(l, 1)(k, device).wait_send()
+            u_tail_copy(l)(k, device).wait_send()
+            for g in range(5):
+                s_copy(l, g)(k, device).wait_send()
+
     send_back(3)
     send_back(2)
 
@@ -631,6 +659,14 @@
     def _():
         relay(0)
         relay(1)
+
+    @pl.when(is_owner)
+    def _():
+        for hop in range(1, 5):
+            for p in range(2):
+                for direction in (UP, DOWN):
+                    if hop < 4 or p == direction:
+                        z_copy(direction, hop, p).wait_send()
 
     send_back(1)
     send_back(0)
@@ -712,10 +748,14 @@
             for t in range(2):
                 rows = slice(t * HALF, (t + 1) * HALF)
                 term = dot_nt(both[rows, :], both)
-                gram_sum[rows, :] = term if hop == 1 else gram_sum[rows, :] + term
-        norm = jnp.sqrt(jnp.sum(squares, axis=1, keepdims=True))
-        inverse = 1.0 / (norm + EPSILON)
-        gram[...] = (gram_sum[...] * inverse * inverse).astype(BF16)
+                if hop > 1:
+                    term = gram_sum[rows, :] + term
+                if hop < 4:
+                    gram_sum[rows, :] = term
+                else:
+                    norm = jnp.sqrt(jnp.sum(squares, axis=1, keepdims=True))
+                    inverse = 1.0 / (norm + EPSILON)
+                    gram[rows, :] = (term * inverse * inverse).astype(BF16)
 
         halves = [slice(0, HALF), slice(HALF, FF)]
         for rows in halves:
@@ -742,61 +782,12 @@
         rows_ref[...] = (QUINT_A * it_rows + dot(poly_rows, x1_ref[...])).astype(BF16)
         for k in range(1, NX):
             rows_copy(k).start()
-        fin[l_own] = rows_ref[pl.ds(aligned(x * 32, 32), 32), :]
-
-    for n in range(1, NY):
-        view = ret.at[chip_rows(wrap(y - REL[n], NY)), :]
-        copy(view, view, rt_s.at[n], rt_r.at[n], peer(dy=-REL[n])).wait_recv()
-
-    def core_rows(core):
-        return pl.ds(aligned(core * TOK, TOK), TOK)
-
-    for_sibling[...] = dot(picked[core_rows(1 - c), :], ret[...])
-    sibling = copy(for_sibling, from_sibling, sib_s, sib_r, peer(dc=1))
-    start(sibling)
-    mine = dot(picked[core_rows(c), :], ret[...])
-    sibling.wait_recv()
-    out_tok[...] = (mine + from_sibling[...]).astype(BF16)
-
-    scale = 0.2 * math.sqrt(max(FF, D))
-    for l in range(2):
-        owner_x = 2 * c + l
-
-        @pl.when(x != owner_x)
-        def _():
-            view = fin.at[l]
-            copy(view, view, fn_s.at[1], fn_r.at[l], peer(dx=1)).wait_recv()
-
-        out_mu[:, l, :] = scale * fin[l, 0:ROWS, :].astype(F32)
-
-    for cp in sent:
-        cp.wait_send()
-
-    for l in range(2):
-        k = wrap(x - 2 * c - l, NX)
-
-        @pl.when(k != 0)
-        def _():
-            device = (z * NX + 2 * c + l, me)
-            w_copy(l)(k, device).wait_send()
-            u_copy(l)(k, device).wait_send()
-            u_tail_copy(l)(k, device).wait_send()
-            for g in range(4):
-                s_copy(l, g)(k, device).wait_send()
-
-    @pl.when(is_owner)
-    def _():
         for d in range(2):
             direct_copy(d).wait_send()
             third_copy(d).wait_send()
             fourth_copy(d).wait_send()
             relayed_copy(d).wait_send()
-
         for hop in range(1, 5):
-            for p in range(2):
-                for direction in (UP, DOWN):
-                    if hop < 4 or p == direction:
-                        z_copy(direction, hop, p).wait_send()
             for p in range(4):
                 for direction in (UP, DOWN):
                     if hop < 4 or p // 2 == direction:
@@ -804,8 +795,45 @@
         for g in range(4):
             for k in range(1, NX):
                 sg_copy(k, g).wait_send()
+        fin[l_own] = rows_ref[pl.ds(aligned(x * 32, 32), 32), :]
+
+    for n in range(1, NY):
+        view = ret.at[chip_rows(wrap(y - REL[n], NY)), :]
+        copy(view, view, rt_s.at[n], rt_r.at[n], peer(dy=-REL[n])).wait_recv()
+
+    def core_rows(core):
+        return pl.ds(aligned(core * TOK, TOK), TOK)
+
+    for_sibling[...] = dot(picked[core_rows(1 - c), :], ret[...])
+    sibling = copy(for_sibling, from_sibling, sib_s, sib_r, peer(dc=1))
+    start(sibling)
+    mine = dot(picked[core_rows(c), :], ret[...])
+    sibling.wait_recv()
+    out_tok[...] = (mine + from_sibling[...]).astype(BF16)
+
+    for l in range(2):
+        owner_x = 2 * c + l
+
+        @pl.when(x != owner_x)
+        def _():
+            view = fin.at[l]
+            copy(view, view, fn_s.at[1], fn_r.at[l], peer(dx=1)).wait_recv()
+
+        out_rows[l] = fin[l]
+
+    drain()
+
+    @pl.when(is_owner)
+    def _():
         for k in range(1, NX):
             rows_copy(k).wait_send()
+
+
+def results(token_ref, rows_ref, out_tok, out_mu):
+    scale = 0.2 * math.sqrt(max(FF, D))
+    out_tok[...] = token_ref[...]
+    for l in range(2):
+        out_mu[:, l, :] = scale * rows_ref[l, 0:ROWS, :].astype(F32)
 
 
 def body(tokens, weights, gate, adjoint, chosen, seat, quota):
@@ -861,10 +889,10 @@
         sem((NX,)),
         sem((2, 4, 2)),
         sem((2, 4, 2)),
-        sem((2, 2)),
-        sem((NX, 2)),
-        sem((2, 4)),
-        sem((NX, 4)),
+        sem((2, 3)),
+        sem((NX, 3)),
+        sem((2, 5)),
+        sem((NX, 5)),
         sem((NX, 4)),
         sem((2, 4)),
         sem((2,)),
@@ -887,11 +915,11 @@
         sem,
         sem,
     ]
-    return pl.pallas_call(
+    token_grad, update_rows = pl.pallas_call(
         kernel,
         out_shape=(
             jax.ShapeDtypeStruct((TOK, D), BF16),
-            jax.ShapeDtypeStruct((ROWS, 2, D), F32),
+            jax.ShapeDtypeStruct((2, 32, D), BF16),
         ),
         in_specs=[anywhere] * 6 + [pl.BlockSpec(memory_space=pltpu.SMEM), anywhere],
         out_specs=(vmem, vmem),
@@ -904,6 +932,17 @@
         ),
         name="expert_backward",
     )(tokens, weights, gate, adjoint, chosen.T, seat.T, quota, jnp.asarray(layout_tables()))
+    return pl.pallas_call(
+        results,
+        out_shape=(
+            jax.ShapeDtypeStruct((TOK, D), BF16),
+            jax.ShapeDtypeStruct((ROWS, 2, D), F32),
+        ),
+        in_specs=[vmem] * 2,
+        out_specs=(vmem, vmem),
+        cost_estimate=pl.CostEstimate(flops=45056, bytes_accessed=10**6, transcendentals=0),
+        name="results",
+    )(token_grad, update_rows)
 
 
 def solution(mesh):

time: 95.2 us -> 93.1 us (0.978); the launches traced: 93.9 us -> 92.9 us
  local copies, waits for them, and re-layouts: 2.38 us -> 0 us
  Pallas kernels: 90.8 us -> 92.3 us
    unnamed x4 -> x0, local copies, waits for them, and re-layouts: 2.38 us -> none
    pallas_call x0 -> x1, Pallas kernels: none -> 1.76 us  [body(): pl.pallas_call(results, out_shape=(jax.ShapeDtypeStruct((TOK, D), BF16),...]
where the time goes in v4:
time: 93.1 us; the launch traced here: 92.9 us
  Pallas kernels  92.3 us (99%)
    pallas_call x1, Pallas kernels, body(): pl.pallas_call(kernel, out_shape=(jax.ShapeDtypeStruct((TOK, D), BF16), j...  90.5 us

profile of v4, /device:TPU:6, one launch (start us, length us, event | category | flops | bytes accessed | tf_op | source)
XLA Modules:
  0.0 92.9 jit_solution(7020048159605660194)
XLA Ops:
  0.6 90.5 %expert_backward.1 = (bf16[128,1024]{1,0:T(8,128)(2,1)}, bf16[2,32,1024]{2,1,0:T(8,128)(2,1)}) custom-call(bf16[128,1024]{1,0:T(8,128)(2,1)} %tok_hbm.1, bf16[22,2,1024]{2,1,0:T(2,128)(2,1)} %w_hbm.1, bf16[704,640]{1,0:T(8,128)(2,1)} %gate_hbm.1, bf16[704,640]{1,0:T(8,128)(2,1)} %adj_hbm.1, s32[6,128]{1,0:T(8,128)} %bitcast.2, s32[6,128]{1,0:T(8,128)} %bitcast.3, ...), custom_call_target="tpu_custom_call" | custom-call | flops 16000000000 | bytes 5000000 | tf_op jit(solution)/shard_map/expert_backward/pallas_call | solution.py:918
  91.1 1.8 %results.1 = (bf16[128,1024]{1,0:T(8,128)(2,1)}, f32[22,2,1024]{2,1,0:T(2,128)}) custom-call(bf16[128,1024]{1,0:T(8,128)(2,1)} %get-tuple-element.4.token_ref, bf16[2,32,1024]{2,1,0:T(8,128)(2,1)} %get-tuple-element.5.rows_ref), custom_call_target="tpu_custom_call" | custom-call | flops 45056 | bytes 1000000 | tf_op jit(solution)/shard_map/results/pallas_call | solution.py:935

commit v5 on v4

--- a/solution.py
+++ b/solution.py
@@ -782,6 +782,29 @@
         rows_ref[...] = (QUINT_A * it_rows + dot(poly_rows, x1_ref[...])).astype(BF16)
         for k in range(1, NX):
             rows_copy(k).start()
+        fin[l_own] = rows_ref[pl.ds(aligned(x * 32, 32), 32), :]
+
+    for n in range(1, NY):
+        view = ret.at[chip_rows(wrap(y - REL[n], NY)), :]
+        copy(view, view, rt_s.at[n], rt_r.at[n], peer(dy=-REL[n])).wait_recv()
+
+    def core_rows(core):
+        return pl.ds(aligned(core * TOK, TOK), TOK)
+
+    left, right = slice(0, D // 2), slice(D // 2, D)
+    sibling = []
+    for h, cols in enumerate((left, right)):
+        for_sibling[:, cols] = dot(picked[core_rows(1 - c), :], ret[:, cols])
+        view = pl.ds(h * (D // 2), D // 2)
+        cp = copy(
+            for_sibling.at[:, view], from_sibling.at[:, view], sib_s.at[h], sib_r.at[h], peer(dc=1)
+        )
+        start(cp)
+        sibling.append(cp)
+    mine = [dot(picked[core_rows(c), :], ret[:, cols]) for cols in (left, right)]
+
+    @pl.when(is_owner)
+    def _():
         for d in range(2):
             direct_copy(d).wait_send()
             third_copy(d).wait_send()
@@ -795,21 +818,10 @@
         for g in range(4):
             for k in range(1, NX):
                 sg_copy(k, g).wait_send()
-        fin[l_own] = rows_ref[pl.ds(aligned(x * 32, 32), 32), :]
-
-    for n in range(1, NY):
-        view = ret.at[chip_rows(wrap(y - REL[n], NY)), :]
-        copy(view, view, rt_s.at[n], rt_r.at[n], peer(dy=-REL[n])).wait_recv()
-
-    def core_rows(core):
-        return pl.ds(aligned(core * TOK, TOK), TOK)
-
-    for_sibling[...] = dot(picked[core_rows(1 - c), :], ret[...])
-    sibling = copy(for_sibling, from_sibling, sib_s, sib_r, peer(dc=1))
-    start(sibling)
-    mine = dot(picked[core_rows(c), :], ret[...])
-    sibling.wait_recv()
-    out_tok[...] = (mine + from_sibling[...]).astype(BF16)
+
+    for h, cols in enumerate((left, right)):
+        sibling[h].wait_recv()
+        out_tok[:, cols] = (mine[h] + from_sibling[:, cols]).astype(BF16)
 
     for l in range(2):
         owner_x = 2 * c + l
@@ -912,8 +924,8 @@
         pltpu.VMEM((2 * TOK, SLOTS), BF16),
         pltpu.VMEM((TOK, D), F32),
         pltpu.VMEM((TOK, D), F32),
-        sem,
-        sem,
+        sem((2,)),
+        sem((2,)),
     ]
     token_grad, update_rows = pl.pallas_call(
         kernel,

time: 93.1 us -> 93.1 us (level)
  no operation moved by 1% of the time
where the time goes in v5:
time: 93.1 us; the launch traced here: 92.9 us
  Pallas kernels  92.3 us (99%)
    pallas_call x1, Pallas kernels, body(): pl.pallas_call(kernel, out_shape=(jax.ShapeDtypeStruct((TOK, D), BF16), j...  90.5 us

profile of v5, /device:TPU:6, one launch (start us, length us, event | category | flops | bytes accessed | tf_op | source)
XLA Modules:
  0.0 92.9 jit_solution(8412212943658801999)
XLA Ops:
  0.6 90.5 %expert_backward.1 = (bf16[128,1024]{1,0:T(8,128)(2,1)}, bf16[2,32,1024]{2,1,0:T(8,128)(2,1)}) custom-call(bf16[128,1024]{1,0:T(8,128)(2,1)} %tok_hbm.1, bf16[22,2,1024]{2,1,0:T(2,128)(2,1)} %w_hbm.1, bf16[704,640]{1,0:T(8,128)(2,1)} %gate_hbm.1, bf16[704,640]{1,0:T(8,128)(2,1)} %adj_hbm.1, s32[6,128]{1,0:T(8,128)} %bitcast.2, s32[6,128]{1,0:T(8,128)} %bitcast.3, ...), custom_call_target="tpu_custom_call" | custom-call | flops 16000000000 | bytes 5000000 | tf_op jit(solution)/shard_map/expert_backward/pallas_call | solution.py:930
  91.2 1.8 %results.1 = (bf16[128,1024]{1,0:T(8,128)(2,1)}, f32[22,2,1024]{2,1,0:T(2,128)}) custom-call(bf16[128,1024]{1,0:T(8,128)(2,1)} %get-tuple-element.4.token_ref, bf16[2,32,1024]{2,1,0:T(8,128)(2,1)} %get-tuple-element.5.rows_ref), custom_call_target="tpu_custom_call" | custom-call | flops 45056 | bytes 1000000 | tf_op jit(solution)/shard_map/results/pallas_call | solution.py:947
